TPU v7x, 768 devices: a whole 4x8x12 slice. The times are simulated.
768 devices in a mesh: dom: 192 (over z, y, core), rep: 4 (over x).
Axes of the slice: x: 4, y: 8, z: 12, core: 2. Of those that a mesh axis runs over, the one named last changes fastest.
Arguments:
- features: bfloat16 [589824, 128], P('dom'), may hold values from -6 to 6
- w_self: bfloat16 [128, 256], replicated, may hold values from -0.5 to 0.5
- w_neigh: bfloat16 [128, 256], replicated, may hold values from -0.5 to 0.5
- bias: float32 [256], replicated, may hold values from -3 to 3
- cotangent: bfloat16 [589824, 256], P(('dom', 'rep')), may hold values from -6 to 6
- slot_source: int32 [4608, 8], P(('dom', 'rep')), may hold values from 0 to 59, as said below
- tile_masks: int32 [4608, 8, 128, 128], P(('dom', 'rep')), may hold values from 0 to 1, as said below
- panel_blocks: int32 [192, 6, 6], P('dom'), may hold values from 0 to 23
Outputs:
- activated: bfloat16 [589824, 256], P(('dom', 'rep'))
- grad_features: float32 [589824, 128], P(('dom', 'rep'))
- grad_self: float32 [128, 256], replicated
- grad_neigh: float32 [128, 256], replicated
- grad_bias: float32 [256], replicated
Inputs may be any that keep to these rules, and one draw needn't show every extreme that they name: `slot_source`: slot 0 of each destination block names the block's own position in its partition; odd slots name received blocks, the other even slots own blocks of the partition. `tile_masks`: some nodes have no edges at all.
All inputs are finite; a program needn't handle non-finite values.
Results may differ from a plain program's by a relative error of at most 0.0047.
Values may be sent and summed in bfloat16 or wider, within the bound.
A program may use at most 64 MiB of HBM per device.

v0:
```python
import math

import jax
import jax.numpy as jnp
from jax import lax
from jax.sharding import PartitionSpec as P


def passed_along(block, axis, distance):
    devices = range(lax.axis_size(axis))
    route = [((i - distance) % len(devices), i) for i in devices]
    return lax.ppermute(block, axis, route)


def per_device(features, w_self, w_neigh, bias, cotangent, slot_source, tile_masks, panel_blocks):
    tile = tile_masks.shape[2]
    dest_blocks = slot_source.shape[0]
    slot_count = slot_source.shape[1]
    in_width = features.shape[1]
    part_blocks = features.shape[0] // tile
    turns = panel_blocks.shape[1]
    panel = panel_blocks.shape[2]
    rows = dest_blocks * tile
    replicas = lax.axis_size("rep")
    rank = lax.axis_index("rep")
    offsets = [t // 2 + 1 if t % 2 == 0 else -(t // 2 + 1) for t in range(turns)]
    own_blocks = features.reshape(part_blocks, tile, in_width)
    received = []
    for turn in range(turns):
        outgoing = own_blocks[panel_blocks[0, turn]]
        received.append(passed_along(outgoing, "dom", offsets[turn]))
    sources = jnp.concatenate([own_blocks] + received, 0)
    tiles = sources[slot_source]
    mask_w = tile_masks.astype(jnp.bfloat16)
    agg_sum = jnp.einsum("dsij,dsjf->dif", mask_w, tiles, preferred_element_type=jnp.float32)
    degree = jnp.maximum(jnp.sum(tile_masks, axis=(1, 3)), 1).astype(jnp.float32).reshape(rows, 1)
    agg = (agg_sum.reshape(rows, in_width) / degree).astype(jnp.bfloat16)
    own_rows = lax.dynamic_slice_in_dim(features, rank * rows, rows, 0)
    z = (
        jnp.dot(own_rows, w_self, preferred_element_type=jnp.float32)
        + jnp.dot(agg, w_neigh, preferred_element_type=jnp.float32)
        + bias
    )
    activated = jax.nn.silu(z).astype(jnp.bfloat16)
    sig = jax.nn.sigmoid(z)
    dz = cotangent.astype(jnp.float32) * (sig * (1.0 + z * (1.0 - sig)))
    dz_b = dz.astype(jnp.bfloat16)
    part_self = jnp.einsum("nf,nh->fh", own_rows, dz_b, preferred_element_type=jnp.float32)
    part_neigh = jnp.einsum("nf,nh->fh", agg, dz_b, preferred_element_type=jnp.float32)
    part_bias = jnp.sum(dz, axis=0)
    total_self, total_neigh, total_bias = lax.psum(
        (part_self, part_neigh, part_bias), ("dom", "rep")
    )
    scale = 1.0 / math.sqrt(rows * replicas * lax.axis_size("dom"))
    q = (
        jnp.einsum("nh,fh->nf", dz_b, w_neigh, preferred_element_type=jnp.float32) / degree
    ).astype(jnp.bfloat16)
    q_blocks = q.reshape(dest_blocks, tile, in_width)
    contrib = jnp.einsum("dsij,dif->dsjf", mask_w, q_blocks, preferred_element_type=jnp.float32)
    source_count = sources.shape[0]
    src_grad = (
        jnp.zeros((source_count, tile, in_width), jnp.float32)
        .at[slot_source.reshape(dest_blocks * slot_count)]
        .add(contrib.reshape(dest_blocks * slot_count, tile, in_width))
    )
    own_grad = src_grad[:part_blocks]
    panel_grad = src_grad[part_blocks:].reshape(turns, panel, tile, in_width)
    for turn in range(turns):
        returned = passed_along(
            panel_grad[turn].astype(jnp.bfloat16), "dom", -offsets[turn]
        ).astype(jnp.float32)
        own_grad = own_grad.at[panel_blocks[0, turn]].add(returned)
    partition_grad = own_grad.reshape(part_blocks * tile, in_width)
    mine = lax.psum_scatter(
        partition_grad.astype(jnp.bfloat16), "rep", scatter_dimension=0, tiled=True
    ).astype(jnp.float32)
    grad_features = jnp.einsum("nh,fh->nf", dz_b, w_self, preferred_element_type=jnp.float32) + mine
    return (activated, grad_features, total_self * scale, total_neigh * scale, total_bias * scale)


def solution(mesh):
    in_specs = (
        P("dom", None),
        P(),
        P(),
        P(),
        P(("dom", "rep"), None),
        P(("dom", "rep"), None),
        P(("dom", "rep"), None, None, None),
        P("dom", None, None),
    )
    out_specs = (P(("dom", "rep"), None), P(("dom", "rep"), None), P(), P(), P())
    return jax.shard_map(
        per_device, mesh=mesh, in_specs=in_specs, out_specs=out_specs, check_vma=False
    )
```

profile of v0, /device:TPU:1, one launch (start us, length us, event | category | flops | bytes accessed | tf_op | source)
XLA Modules:
  0.0 594.3 jit_solution(11783085683294469411)
XLA Ops:
  8.0 0.0 all-reduce.3.cloned.1.call-start
  8.1 0.8 fusion.16
  8.9 1.7 gather_fusion
  10.6 4.6 collective-permute-start
  15.2 1.7 gather_fusion.1
  17.0 9.8 %collective-permute-start.1 = (bf16[6,128,128]{2,1,0:T(8,128)(2,1)S(1)}, bf16[6,128,128]{2,1,0:T(8,128)(2,1)S(1)}, u32[]{:S(2)}, u32[]{:S(2)}) collective-permute-start(bf16[6,128,128]{2,1,0:T(8,128)(2,1)S(1)} %gather_fusion.1), channel_id=1, source_target_pairs={{4,0},{8,4},{12,8},{16,12},{20,16},{24,20},{28,24},{32,28},{36,32}... | collective-permute-start | bytes 589832 | tf_op jit(solution)/shard_map/ppermute | solution.py:12
  26.7 1.7 gather_fusion.2
  28.5 1.9 collective-permute-start.2
  30.4 1.7 gather_fusion.3
  32.1 8.2 %collective-permute-start.3 = (bf16[6,128,128]{2,1,0:T(8,128)(2,1)S(1)}, bf16[6,128,128]{2,1,0:T(8,128)(2,1)S(1)}, u32[]{:S(2)}, u32[]{:S(2)}) collective-permute-start(bf16[6,128,128]{2,1,0:T(8,128)(2,1)S(1)} %gather_fusion.3), channel_id=1, source_target_pairs={{8,0},{12,4},{16,8},{20,12},{24,16},{28,20},{32,24},{36,28},{40,32... | collective-permute-start | bytes 589832 | tf_op jit(solution)/shard_map/ppermute | solution.py:12
  40.4 1.7 gather_fusion.4
  42.1 1.9 collective-permute-start.4
  44.1 0.1 reshape.249
  44.2 1.3 gather_fusion.5
  45.4 0.1 reshape.302
  45.5 2.1 reduce_sum.18
  47.6 1.1 fusion.9
  48.8 0.9 constant_dynamic-update-slice_fusion.6
  49.7 7.0 %collective-permute-start.5 = (bf16[6,128,128]{2,1,0:T(8,128)(2,1)}, bf16[6,128,128]{2,1,0:T(8,128)(2,1)S(1)}, u32[]{:S(2)}, u32[]{:S(2)}) collective-permute-start(bf16[6,128,128]{2,1,0:T(8,128)(2,1)} %gather_fusion.5), channel_id=1, source_target_pairs={{12,0},{16,4},{20,8},{24,12},{28,16},{32,20},{36,24},{40,28},{44,3... | collective-permute-start | bytes 589832 | tf_op jit(solution)/shard_map/ppermute | solution.py:12
  56.7 0.7 constant_dynamic-update-slice_fusion.5
  57.4 0.7 constant_dynamic-update-slice_fusion.4
  58.1 0.7 constant_dynamic-update-slice_fusion.3
  58.8 0.7 constant_dynamic-update-slice_fusion.2
  59.5 1.8 constant_dynamic-update-slice_fusion.1
  61.2 0.7 constant_dynamic-update-slice_fusion
  61.9 3.5 gather_fusion.6
  65.4 2.1 fusion.4
  67.5 0.2 fusion.6
  67.7 1.3 fusion.20
  69.0 0.7 copy-done.3
  69.7 0.3 fusion.1
  70.0 2.3 fusion.2
  72.3 2.4 copy.14
  74.7 2.4 broadcast_in_dim.5
  77.1 9.1 %scatter_fusion = f32[60,128,128]{2,1,0:T(8,128)} fusion(f32[60,128,128]{2,1,0:T(8,128)} %broadcast_in_dim.5, s32[48]{0:T(128)S(1)} %fusion.17, f32[48,128,128]{2,1,0:T(8,128)S(1)} %copy.14), kind=kCustom, calls=%fused_computation.7 | custom fusion | flops 786432 | bytes 9437376 | tf_op jit(solution)/shard_map/scatter-add | solution.py:64
  86.1 2.4 convert.8
  88.6 0.8 fusion.21
  89.4 7.8 %collective-permute-start.6 = (bf16[6,128,128]{2,1,0:T(8,128)(2,1)S(1)}, bf16[6,128,128]{2,1,0:T(8,128)(2,1)S(1)}, u32[]{:S(2)}, u32[]{:S(2)}) collective-permute-start(bf16[6,128,128]{2,1,0:T(8,128)(2,1)S(1)} %get-tuple-element.14), channel_id=1, source_target_pairs={{4,0},{8,4},{12,8},{16,12},{20,16},{24,20},{28,24},{32,28},{36,32}... | collective-permute-start | bytes 589832 | tf_op jit(solution)/shard_map/ppermute | solution.py:12
  97.1 1.9 collective-permute-start.7
  99.1 6.9 %collective-permute-start.8 = (bf16[6,128,128]{2,1,0:T(8,128)(2,1)S(1)}, bf16[6,128,128]{2,1,0:T(8,128)(2,1)}, u32[]{:S(2)}, u32[]{:S(2)}) collective-permute-start(bf16[6,128,128]{2,1,0:T(8,128)(2,1)S(1)} %get-tuple-element.12), channel_id=1, source_target_pairs={{8,0},{12,4},{16,8},{20,12},{24,16},{28,20},{32,24},{36,28},{40,32... | collective-permute-start | bytes 589832 | tf_op jit(solution)/shard_map/ppermute | solution.py:12
  106.0 1.9 collective-permute-start.9
  107.9 7.4 %collective-permute-start.10 = (bf16[6,128,128]{2,1,0:T(8,128)(2,1)S(1)}, bf16[6,128,128]{2,1,0:T(8,128)(2,1)}, u32[]{:S(2)}, u32[]{:S(2)}) collective-permute-start(bf16[6,128,128]{2,1,0:T(8,128)(2,1)S(1)} %get-tuple-element.10), channel_id=1, source_target_pairs={{12,0},{16,4},{20,8},{24,12},{28,16},{32,20},{36,24},{40,28},{44,3... | collective-permute-start | bytes 589832 | tf_op jit(solution)/shard_map/ppermute | solution.py:12
  115.3 0.9 fusion.22
  116.3 1.9 collective-permute-start.11
  118.2 1.8 fusion.7
  120.0 0.0 reduce-scatter.2.cloned.1.call-start
  120.1 1.5 slice.91
  121.6 1.0 convert_element_type.69
  122.6 1.1 scatter_fusion.1
  123.7 1.0 convert_element_type.70
  124.6 1.1 scatter_fusion.2
  125.7 1.0 convert_element_type.71
  126.7 1.1 scatter_fusion.3
  127.8 1.0 convert_element_type.72
  128.7 1.1 scatter_fusion.4
  129.8 1.0 convert_element_type.73
  130.8 1.1 scatter_fusion.5
  131.9 1.1 scatter_fusion.6
  133.0 1.0 convert_element_type.75
  134.0 110.4 %psum.23 = f32[256]{0:T(256)S(1)} all-reduce(f32[256]{0:T(256)S(1)} %get-tuple-element.7), channel_id=1, replica_groups=mesh['dom'=192,'rep'=4] {'dom','rep'}, use_global_device_ids=true, to_apply=%region_12.13 | all-reduce | flops 256 | bytes 2048 | tf_op jit(solution)/shard_map/psum | solution.py:51
  244.4 0.6 broadcast_multiply_fusion.2
  244.9 338.2 %all-reduce.3.cloned.1.call-done = (f32[128,256]{1,0:T(8,128)}, f32[128,256]{1,0:T(8,128)}) async-done(((f32[128,256]{1,0:T(8,128)}, f32[128,256]{1,0:T(8,128)}), (f32[128,256]{1,0:T(8,128)}, f32[128,256]{1,0:T(8,128)})) %all-reduce.3.cloned.1.call-update) | async-done | bytes 262160 | tf_op jit(solution)/shard_map/psum | solution.py:51
  583.2 1.7 broadcast_multiply_fusion
  584.9 1.9 convolution_add_fusion.1
  (47 shorter events, 0.2 us)
Async XLA Ops:
  8.0 59.7 %copy-start = (bf16[128,256]{1,0:T(8,128)(2,1)S(1)}, bf16[128,256]{1,0:T(8,128)(2,1)}, u32[]{:S(2)}) copy-start(bf16[128,256]{1,0:T(8,128)(2,1)} %param.10) | copy-start | bytes 196612
  8.0 36.2 %copy-start.2 = (bf16[3072,128]{1,0:T(8,128)(2,1)S(1)}, bf16[3072,128]{1,0:T(8,128)(2,1)}, u32[]{:S(2)}) copy-start(bf16[3072,128]{1,0:T(8,128)(2,1)} %param.8) | copy-start | bytes 2359300
  8.0 36.0 %copy-start.8 = (s32[6,8]{1,0:T(8,128)S(1)}, s32[6,8]{1,0:T(8,128)}, u32[]{:S(2)}) copy-start(s32[6,8]{1,0:T(8,128)} %param.13) | copy-start | bytes 580
  8.0 575.2 %all-reduce.3.cloned.1.call-start = ((), (), s32[]{:S(2)}) async-start(), calls=%async_computation.2 | async-start | bytes 524288 | tf_op jit(solution)/shard_map/psum | solution.py:51
  10.6 39.1 %collective-permute-start = (bf16[6,128,128]{2,1,0:T(8,128)(2,1)S(1)}, bf16[6,128,128]{2,1,0:T(8,128)(2,1)S(1)}, u32[]{:S(2)}, u32[]{:S(2)}) collective-permute-start(bf16[6,128,128]{2,1,0:T(8,128)(2,1)S(1)} %gather_fusion), channel_id=1, source_target_pairs={{764,0},{0,4},{4,8},{8,12},{12,16},{16,20},{20,24},{24,28},{28,32}... | collective-permute-start | bytes 589832 | tf_op jit(solution)/shard_map/ppermute | solution.py:12
  17.0 40.4 %collective-permute-start.1 = (bf16[6,128,128]{2,1,0:T(8,128)(2,1)S(1)}, bf16[6,128,128]{2,1,0:T(8,128)(2,1)S(1)}, u32[]{:S(2)}, u32[]{:S(2)}) collective-permute-start(bf16[6,128,128]{2,1,0:T(8,128)(2,1)S(1)} %gather_fusion.1), channel_id=1, source_target_pairs={{4,0},{8,4},{12,8},{16,12},{20,16},{24,20},{28,24},{32,28},{36,32}... | collective-permute-start | bytes 589832 | tf_op jit(solution)/shard_map/ppermute | solution.py:12
  28.5 29.6 %collective-permute-start.2 = (bf16[6,128,128]{2,1,0:T(8,128)(2,1)S(1)}, bf16[6,128,128]{2,1,0:T(8,128)(2,1)S(1)}, u32[]{:S(2)}, u32[]{:S(2)}) collective-permute-start(bf16[6,128,128]{2,1,0:T(8,128)(2,1)S(1)} %gather_fusion.2), channel_id=1, source_target_pairs={{760,0},{764,4},{0,8},{4,12},{8,16},{12,20},{16,24},{20,28},{24,32... | collective-permute-start | bytes 589832 | tf_op jit(solution)/shard_map/ppermute | solution.py:12
  32.1 26.6 %collective-permute-start.3 = (bf16[6,128,128]{2,1,0:T(8,128)(2,1)S(1)}, bf16[6,128,128]{2,1,0:T(8,128)(2,1)S(1)}, u32[]{:S(2)}, u32[]{:S(2)}) collective-permute-start(bf16[6,128,128]{2,1,0:T(8,128)(2,1)S(1)} %gather_fusion.3), channel_id=1, source_target_pairs={{8,0},{12,4},{16,8},{20,12},{24,16},{28,20},{32,24},{36,28},{40,32... | collective-permute-start | bytes 589832 | tf_op jit(solution)/shard_map/ppermute | solution.py:12
  40.4 7.3 %copy-start.6 = (bf16[128,256]{1,0:T(8,128)(2,1)S(1)}, bf16[128,256]{1,0:T(8,128)(2,1)}, u32[]{:S(2)}) copy-start(bf16[128,256]{1,0:T(8,128)(2,1)} %param.9) | copy-start | bytes 196612
  42.1 17.3 %collective-permute-start.4 = (bf16[6,128,128]{2,1,0:T(8,128)(2,1)S(1)}, bf16[6,128,128]{2,1,0:T(8,128)(2,1)}, u32[]{:S(2)}, u32[]{:S(2)}) collective-permute-start(bf16[6,128,128]{2,1,0:T(8,128)(2,1)S(1)} %gather_fusion.4), channel_id=1, source_target_pairs={{756,0},{760,4},{764,8},{0,12},{4,16},{8,20},{12,24},{16,28},{20,3... | collective-permute-start | bytes 589832 | tf_op jit(solution)/shard_map/ppermute | solution.py:12
  49.7 11.5 %collective-permute-start.5 = (bf16[6,128,128]{2,1,0:T(8,128)(2,1)}, bf16[6,128,128]{2,1,0:T(8,128)(2,1)S(1)}, u32[]{:S(2)}, u32[]{:S(2)}) collective-permute-start(bf16[6,128,128]{2,1,0:T(8,128)(2,1)} %gather_fusion.5), channel_id=1, source_target_pairs={{12,0},{16,4},{20,8},{24,12},{28,16},{32,20},{36,24},{40,28},{44,3... | collective-permute-start | bytes 589832 | tf_op jit(solution)/shard_map/ppermute | solution.py:12
  59.5 5.9 copy-start.1
  65.4 2.3 copy-start.5
  65.4 2.3 copy-start.9
  65.4 2.3 copy-start.10
  69.0 0.7 copy-start.3
  88.6 26.7 %copy-start.4 = (bf16[768,256]{1,0:T(8,128)(2,1)S(1)}, bf16[768,256]{1,0:T(8,128)(2,1)}, u32[]{:S(2)}) copy-start(bf16[768,256]{1,0:T(8,128)(2,1)} %copy-done.3) | copy-start | bytes 1179652
  89.4 26.9 %collective-permute-start.6 = (bf16[6,128,128]{2,1,0:T(8,128)(2,1)S(1)}, bf16[6,128,128]{2,1,0:T(8,128)(2,1)S(1)}, u32[]{:S(2)}, u32[]{:S(2)}) collective-permute-start(bf16[6,128,128]{2,1,0:T(8,128)(2,1)S(1)} %get-tuple-element.14), channel_id=1, source_target_pairs={{4,0},{8,4},{12,8},{16,12},{20,16},{24,20},{28,24},{32,28},{36,32}... | collective-permute-start | bytes 589832 | tf_op jit(solution)/shard_map/ppermute | solution.py:12
  97.1 26.5 %collective-permute-start.7 = (bf16[6,128,128]{2,1,0:T(8,128)(2,1)}, bf16[6,128,128]{2,1,0:T(8,128)(2,1)}, u32[]{:S(2)}, u32[]{:S(2)}) collective-permute-start(bf16[6,128,128]{2,1,0:T(8,128)(2,1)} %get-tuple-element.13), channel_id=1, source_target_pairs={{764,0},{0,4},{4,8},{8,12},{12,16},{16,20},{20,24},{24,28},{28,32}... | collective-permute-start | bytes 589832 | tf_op jit(solution)/shard_map/ppermute | solution.py:12
  99.1 26.6 %collective-permute-start.8 = (bf16[6,128,128]{2,1,0:T(8,128)(2,1)S(1)}, bf16[6,128,128]{2,1,0:T(8,128)(2,1)}, u32[]{:S(2)}, u32[]{:S(2)}) collective-permute-start(bf16[6,128,128]{2,1,0:T(8,128)(2,1)S(1)} %get-tuple-element.12), channel_id=1, source_target_pairs={{8,0},{12,4},{16,8},{20,12},{24,16},{28,20},{32,24},{36,28},{40,32... | collective-permute-start | bytes 589832 | tf_op jit(solution)/shard_map/ppermute | solution.py:12
  106.0 21.8 %collective-permute-start.9 = (bf16[6,128,128]{2,1,0:T(8,128)(2,1)S(1)}, bf16[6,128,128]{2,1,0:T(8,128)(2,1)}, u32[]{:S(2)}, u32[]{:S(2)}) collective-permute-start(bf16[6,128,128]{2,1,0:T(8,128)(2,1)S(1)} %get-tuple-element.11), channel_id=1, source_target_pairs={{760,0},{764,4},{0,8},{4,12},{8,16},{12,20},{16,24},{20,28},{24,32... | collective-permute-start | bytes 589832 | tf_op jit(solution)/shard_map/ppermute | solution.py:12
  107.9 21.9 %collective-permute-start.10 = (bf16[6,128,128]{2,1,0:T(8,128)(2,1)S(1)}, bf16[6,128,128]{2,1,0:T(8,128)(2,1)}, u32[]{:S(2)}, u32[]{:S(2)}) collective-permute-start(bf16[6,128,128]{2,1,0:T(8,128)(2,1)S(1)} %get-tuple-element.10), channel_id=1, source_target_pairs={{12,0},{16,4},{20,8},{24,12},{28,16},{32,20},{36,24},{40,28},{44,3... | collective-permute-start | bytes 589832 | tf_op jit(solution)/shard_map/ppermute | solution.py:12
  116.2 3.8 copy-start.7
  116.3 15.6 %collective-permute-start.11 = (bf16[6,128,128]{2,1,0:T(8,128)(2,1)S(1)}, bf16[6,128,128]{2,1,0:T(8,128)(2,1)S(1)}, u32[]{:S(2)}, u32[]{:S(2)}) collective-permute-start(bf16[6,128,128]{2,1,0:T(8,128)(2,1)S(1)} %get-tuple-element.9), channel_id=1, source_target_pairs={{756,0},{760,4},{764,8},{0,12},{4,16},{8,20},{12,24},{16,28},{20,3... | collective-permute-start | bytes 589832 | tf_op jit(solution)/shard_map/ppermute | solution.py:12
  120.0 464.9 %reduce-scatter.2.cloned.1.call-start = ((), (), s32[]{:S(2)}) async-start(), calls=%async_computation.1 | async-start | bytes 983040 | tf_op jit(solution)/shard_map/reduce_scatter | solution.py:74
Sparse Core Ops, SparseCore 0:
  120.2 462.9 all-reduce.2
Sparse Core Ops, SparseCore 1:
  134.1 24.3 reduce-scatter.1
where the time goes:
time: 596 us; the launch traced here: 594 us
  waiting for transfers between devices  338 us (57%)
  blocking collectives  110 us (18%)
  starting transfers between devices  61.3 us (10%)
  other arithmetic  29.2 us (5%)
  local copies, waits for them, and re-layouts  27.4 us (5%)
  between operations  16 us (3%)
  matrix products  11.7 us (2%)
    psum x1, waiting for transfers between devices, per_device(): lax.psum((part_self, part_neigh, part_bias), ('dom', 'rep'))  338 us
    psum x1, blocking collectives, per_device(): lax.psum((part_self, part_neigh, part_bias), ('dom', 'rep'))  110 us
    ppermute x12, starting transfers between devices, passed_along(): return lax.ppermute(block, axis, route)  61.2 us
  transfers between devices with their start and end apart: 14, of which 1 were waited for; matrix products, arithmetic and copies ran while one was open for 6% of the time, Pallas kernels for 0%

commit v1 on v0

v1 whole, which is shorter than its diff:
```python
import functools
import math

import jax
import jax.numpy as jnp
from jax import lax
from jax.experimental import pallas as pl
from jax.experimental.pallas import tpu as pltpu
from jax.sharding import PartitionSpec as P

MESH = pl.DeviceIdType.MESH
F32 = jnp.float32
BF16 = jnp.bfloat16
CONTRACT_ROWS = (((0,), (0,)), ((), ()))
CONTRACT_LANES = (((1,), (1,)), ((), ()))


def dot(a, b):
    return jnp.dot(a, b, preferred_element_type=F32)


def chain(values):
    lane = lax.broadcasted_iota(jnp.int32, (1, 128), 1)
    listed = jnp.full((1, 128), -1, jnp.int32)
    for j, value in enumerate(values):
        listed = jnp.where(lane == j, value, listed)
    prev = jnp.zeros((1, 128), jnp.int32)
    last = jnp.zeros((1, 128), jnp.int32)
    for i, value in enumerate(values):
        prev = jnp.where((listed == value) & (lane > i), i + 1, prev)
        last = jnp.where(lane == value, i + 1, last)
    return prev, last


def kernel(
    sizes, feat_hbm, w_self_hbm, w_neigh_hbm, bias_hbm, cot_hbm, masks_hbm, slot_ref, panel_ref,
    act_hbm, gf_hbm, gs_ref, gn_ref, gb_ref,
    feat, w_self, w_neigh, bias, cot, masks, mask_b, mask_t, inv, z0, agg_even, agg_b, dz_b, q_b, act, gf,
    panel_out, recv, grad_out, returned, chain_odd, chain_even, chain_back, own, own_mine, x_pass, x_near,
    got_pass, got_near, idx_v, idx_s,
    r1_out, r1_in, r2_out, r2_in, r3_out, r3_in, r4, r5,
    in_sem, mask_sem, idx_sem, out_sem, fwd_send, fwd_recv, back_send, back_recv, x_send, x_recv,
    s1_send, s1_recv, s2_send, s2_recv, s3_send, s3_recv, s4_send, s4_recv, s5_send, s5_recv,
):
    doms, reps, subs, offsets, nodes = sizes
    layers = doms // subs
    turns = len(offsets)
    panel = panel_ref.shape[2]
    blocks, slots = slot_ref.shape
    half = slots // 2
    part_blocks, tile, width = feat.shape
    hidden = w_self.shape[1]
    rows_each = width // subs
    dom = lax.axis_index("dom")
    rep = lax.axis_index("rep")
    layer = dom // subs
    sub = dom % subs

    def received(i, k):
        return jnp.maximum(slot_ref[i, 2 * k + 1] - part_blocks, 0)

    loads = [
        pltpu.make_async_copy(feat_hbm, feat, in_sem.at[0]),
        pltpu.make_async_copy(w_self_hbm, w_self, in_sem.at[1]),
        pltpu.make_async_copy(w_neigh_hbm, w_neigh, in_sem.at[2]),
        pltpu.make_async_copy(bias_hbm, bias, in_sem.at[3]),
        pltpu.make_async_copy(cot_hbm, cot, in_sem.at[4]),
    ]
    for load in loads:
        load.start()
    for i in range(blocks):
        pltpu.make_async_copy(masks_hbm.at[i], masks.at[i], mask_sem.at[i]).start()

    barrier = pltpu.get_barrier_semaphore()

    def greet(d, r):
        pl.semaphore_signal(barrier, inc=1, device_id=(d, r), device_id_type=MESH)

    for offset in offsets:
        greet((dom + offset + doms) % doms, rep)
    for k in range(1, reps):
        greet(dom, (rep + k) % reps)

    def greet_sub(k, carry):
        greet(layer * subs + (sub + k) % subs, rep)
        return carry

    def greet_layer(k, carry):
        greet(((layer + k) % layers) * subs + sub, rep)
        return carry

    lax.fori_loop(1, subs, greet_sub, 0)
    lax.fori_loop(1, layers, greet_layer, 0)

    loads[0].wait()
    for t in range(turns):
        for i in range(panel):
            panel_out[t * panel + i] = feat[panel_ref[0, t, i]]
    pl.semaphore_wait(barrier, turns + reps - 1 + subs - 1 + layers - 1)

    def to_dom(t, source, target, send, recv_sem, offset):
        part = pl.ds(t * panel, panel)
        return pltpu.make_async_remote_copy(
            src_ref=source.at[part], dst_ref=target.at[part], send_sem=send.at[t], recv_sem=recv_sem.at[t],
            device_id=((dom + offset + doms) % doms, rep), device_id_type=MESH,
        )

    sends = [to_dom(t, panel_out, recv, fwd_send, fwd_recv, offsets[t]) for t in range(turns)]
    for t in reversed(range(turns)):
        sends[t].start()

    odd = [received(i, k) for i in range(blocks) for k in range(half)]
    even = [slot_ref[i, 2 * k] for i in range(blocks) for k in range(half)]
    back = [panel_ref[0, t, i] for t in range(turns) for i in range(panel)]
    for at, values in enumerate((odd, even, back)):
        prev, last = chain(values)
        idx_v[2 * at : 2 * at + 1, :] = prev
        idx_v[2 * at + 1 : 2 * at + 2, :] = last
    idx_v[6:8, :] = jnp.zeros((2, 128), jnp.int32)
    idx_copy = pltpu.make_async_copy(idx_v, idx_s, idx_sem)
    idx_copy.start()
    chain_odd[0] = jnp.zeros((tile, width), F32)
    chain_even[0] = jnp.zeros((tile, width), F32)
    chain_back[0] = jnp.zeros((tile, width), F32)
    loads[1].wait()
    loads[2].wait()
    loads[3].wait()

    def prepare(i, carry):
        pltpu.make_async_copy(masks_hbm.at[i], masks.at[i], mask_sem.at[i]).wait()
        total = jnp.zeros((tile, tile), F32)
        aggregate = jnp.zeros((tile, width), F32)
        for k in range(slots):
            mask = masks[i, k].astype(F32)
            total = total + mask
            mask = mask.astype(BF16)
            mask_b[i, k] = mask
            mask_t[i, k] = mask.T
            if k % 2 == 0:
                aggregate = aggregate + dot(mask, feat[slot_ref[i, k]])
        agg_even[i] = aggregate
        degree = jnp.maximum(jnp.sum(total, axis=1, keepdims=True), 1.0)
        inv[i] = jnp.broadcast_to(1.0 / degree, (tile, width))
        z0[i] = dot(feat[rep * blocks + i], w_self[...]) + bias[...]
        return carry

    lax.fori_loop(0, blocks, prepare, 0)
    loads[4].wait()
    idx_copy.wait()
    for send in sends:
        send.wait_recv()

    def forward(i, bias_total):
        aggregate = agg_even[i]
        for k in range(half):
            aggregate = aggregate + dot(mask_b[i, 2 * k + 1], recv[received(i, k)])
        agg = (aggregate * inv[i]).astype(BF16)
        agg_b[i] = agg
        z = z0[i] + dot(agg, w_neigh[...])
        sig = lax.logistic(z)
        act[i] = (z * sig).astype(BF16)
        dz = cot[i].astype(F32) * (sig * (1.0 + z * (1.0 - sig)))
        dzb = dz.astype(BF16)
        dz_b[i] = dzb
        q = lax.dot_general(dzb, w_neigh[...], CONTRACT_LANES, preferred_element_type=F32)
        q = (q * inv[i]).astype(BF16)
        q_b[i] = q
        for k in range(half):
            at = i * half + k
            chain_odd[at + 1] = chain_odd[idx_s[0, at]] + dot(mask_t[i, 2 * k + 1], q)
        return bias_total + jnp.sum(dz, axis=0, keepdims=True)

    bias_total = lax.fori_loop(0, blocks, forward, jnp.zeros((1, hidden), F32))
    act_copy = pltpu.make_async_copy(act, act_hbm, out_sem.at[0])
    act_copy.start()
    returns = [to_dom(t, grad_out, returned, back_send, back_recv, -offsets[t]) for t in range(turns)]
    for t in reversed(range(turns)):
        for i in range(panel):
            grad_out[t * panel + i] = chain_odd[idx_s[1, t * panel + i]].astype(BF16)
        returns[t].start()

    bias_rows = 8

    def weights(i, carry):
        part_self, part_neigh = carry
        dzb = dz_b[i]
        part_self = part_self + lax.dot_general(
            feat[rep * blocks + i], dzb, CONTRACT_ROWS, preferred_element_type=F32
        )
        part_neigh = part_neigh + lax.dot_general(agg_b[i], dzb, CONTRACT_ROWS, preferred_element_type=F32)
        return part_self, part_neigh

    zero = jnp.zeros((width, hidden), F32)
    part_self, part_neigh = lax.fori_loop(0, blocks, weights, (zero, zero))
    for at, part in enumerate((part_self, part_neigh)):
        for c in range(2):
            r1_out[2 * at + c, 0:width] = part[:, c * 128 : (c + 1) * 128]
    row = lax.broadcasted_iota(jnp.int32, (bias_rows, 128), 0)
    bias_tile = jnp.where(row == 0, bias_total[:, :128], jnp.where(row == 1, bias_total[:, 128:], 0.0))
    for at in range(reps):
        r1_out[at, width : width + bias_rows] = bias_tile

    def stage_1(k):
        peer = (rep + k) % reps
        return pltpu.make_async_remote_copy(
            src_ref=r1_out.at[peer], dst_ref=r1_in.at[k - 1], send_sem=s1_send.at[k - 1], recv_sem=s1_recv.at[k - 1],
            device_id=(dom, peer), device_id_type=MESH,
        )

    for k in range(1, reps):
        stage_1(k).start()

    def backward(i, carry):
        q = q_b[i]
        for k in range(half):
            at = i * half + k
            chain_even[at + 1] = chain_even[idx_s[2, at]] + dot(mask_t[i, 2 * k], q)
        gf[i] = lax.dot_general(dz_b[i], w_self[...], CONTRACT_LANES, preferred_element_type=F32)
        return carry

    lax.fori_loop(0, blocks, backward, 0)

    for k in range(1, reps):
        stage_1(k).wait_recv()
    summed = r1_out[rep]
    for k in range(1, reps):
        summed = summed + r1_in[k - 1]
    for j in range(subs):
        r2_out[j, 0:rows_each] = summed[j * rows_each : (j + 1) * rows_each]
        r2_out[j, rows_each : rows_each + bias_rows] = summed[width : width + bias_rows]

    def stage_2(k):
        peer = (sub + k) % subs
        return pltpu.make_async_remote_copy(
            src_ref=r2_out.at[peer], dst_ref=r2_in.at[k - 1], send_sem=s2_send.at[k - 1], recv_sem=s2_recv.at[k - 1],
            device_id=(layer * subs + peer, rep), device_id_type=MESH,
        )

    def stage_3(k):
        peer = (layer + k) % layers
        return pltpu.make_async_remote_copy(
            src_ref=r3_out, dst_ref=r3_in.at[k - 1], send_sem=s3_send.at[k - 1], recv_sem=s3_recv.at[k - 1],
            device_id=(peer * subs + sub, rep), device_id_type=MESH,
        )

    def stage_4(k):
        peer = (sub + k) % subs
        return pltpu.make_async_remote_copy(
            src_ref=r4.at[sub], dst_ref=r4.at[sub], send_sem=s4_send.at[k - 1], recv_sem=s4_recv.at[k - 1],
            device_id=(layer * subs + peer, rep), device_id_type=MESH,
        )

    def stage_5(k):
        peer = (rep + k) % reps
        return pltpu.make_async_remote_copy(
            src_ref=r5.at[rep], dst_ref=r5.at[rep], send_sem=s5_send.at[k - 1], recv_sem=s5_recv.at[k - 1],
            device_id=(dom, peer), device_id_type=MESH,
        )

    def start_all(stage, count):
        def step(k, carry):
            stage(k).start()
            return carry

        lax.fori_loop(1, count, step, 0)

    def receive_all(stage, count):
        def step(k, carry):
            stage(k).wait_recv()
            return carry

        lax.fori_loop(1, count, step, 0)

    def finish_all(stage, count):
        def step(k, carry):
            stage(k).wait_send()
            return carry

        lax.fori_loop(1, count, step, 0)

    start_all(stage_2, subs)
    receive_all(stage_2, subs)
    summed = r2_out[sub]
    for k in range(1, subs):
        summed = summed + r2_in[k - 1]
    r3_out[...] = summed
    start_all(stage_3, layers)

    def take(t):
        returns[t].wait_recv()
        for i in range(panel):
            at = t * panel + i
            chain_back[at + 1] = chain_back[idx_s[4, at]] + returned[at].astype(F32)

    order = list(range(turns))
    for t in order[: turns // 2]:
        take(t)
    receive_all(stage_3, layers)
    summed = r3_out[...]
    for k in range(1, layers):
        summed = summed + r3_in[k - 1]
    r4[sub] = summed[0:rows_each]
    final_bias = summed[rows_each : rows_each + bias_rows]
    start_all(stage_4, subs)
    for t in order[turns // 2 :]:
        take(t)

    right, left, across = (rep + 1) % reps, (rep + 3) % reps, (rep + 2) % reps
    part = blocks // 2

    def owned(block):
        return chain_even[idx_s[3, block]] + chain_back[idx_s[5, block]]

    def to_rep(source, target, at, peer):
        return pltpu.make_async_remote_copy(
            src_ref=source, dst_ref=target, send_sem=x_send.at[at], recv_sem=x_recv.at[at],
            device_id=(dom, peer), device_id_type=MESH,
        )

    passing = [to_rep(x_pass.at[s], got_pass.at[s], s, (right, left)[s]) for s in range(2)]
    for s in range(2):
        for j in range(part):
            x_pass[s, j] = owned(across * blocks + s * part + j).astype(BF16)
        passing[s].start()
    near = [
        [to_rep(x_near.at[s, h], got_near.at[s, h], 2 + 2 * s + h, (right, left)[s]) for h in range(2)]
        for s in range(2)
    ]
    for s in range(2):
        peer = (right, left)[s]
        for j in range(part):
            x_near[s, 0, j] = owned(peer * blocks + (1 - s) * part + j).astype(BF16)
        near[s][0].start()
    for s in range(2):
        peer = (right, left)[s]
        for j in range(part):
            own[s, j] = owned(peer * blocks + s * part + j)
    for s in range(2):
        passing[s].wait_recv()
        for j in range(part):
            x_near[s, 1, j] = (own[s, j] + got_pass[s, j].astype(F32)).astype(BF16)
        near[s][1].start()
    for j in range(blocks):
        own_mine[j] = owned(rep * blocks + j) + gf[j]

    receive_all(stage_4, subs)
    for j in range(subs):
        r5[rep, j * rows_each : (j + 1) * rows_each] = r4[j]
    for k in range(1, reps):
        stage_5(k).start()

    for s in range(2):
        near[s][0].wait_recv()
    for s in range(2):
        near[s][1].wait_recv()
    for s in range(2):
        for j in range(part):
            at = s * part + j
            gf[at] = own_mine[at] + got_near[0, 1 - s, j].astype(F32) + got_near[1, s, j].astype(F32)
    gf_copy = pltpu.make_async_copy(gf, gf_hbm, out_sem.at[1])
    gf_copy.start()

    scale = 1.0 / math.sqrt(nodes)
    for k in range(1, reps):
        stage_5(k).wait_recv()
    for c in range(2):
        gs_ref[:, c * 128 : (c + 1) * 128] = r5[c] * scale
        gn_ref[:, c * 128 : (c + 1) * 128] = r5[2 + c] * scale
        gb_ref[:, c * 128 : (c + 1) * 128] = final_bias[c : c + 1] * scale

    for send in sends + returns:
        send.wait_send()
    for s in range(2):
        passing[s].wait_send()
        for h in range(2):
            near[s][h].wait_send()
    finish_all(stage_1, reps)
    finish_all(stage_2, subs)
    finish_all(stage_3, layers)
    finish_all(stage_4, subs)
    finish_all(stage_5, reps)
    act_copy.wait()
    gf_copy.wait()


def per_device(sizes, features, w_self, w_neigh, bias, cotangent, slot_source, tile_masks, panel_blocks):
    doms, reps, subs, offsets, nodes = sizes
    layers = doms // subs
    blocks, slots, tile, _ = tile_masks.shape
    width, hidden = w_self.shape
    part_blocks = features.shape[0] // tile
    turns, panel = panel_blocks.shape[1:]
    tiles = blocks * slots // 2
    rows_each = width // subs
    part = blocks // 2
    dma = pltpu.SemaphoreType.DMA
    any_space = pl.BlockSpec(memory_space=pl.ANY)
    vmem = pl.BlockSpec(memory_space=pltpu.VMEM)
    smem = pl.BlockSpec(memory_space=pltpu.SMEM)
    block = (tile, width)
    scratch = [
        pltpu.VMEM((part_blocks,) + block, BF16),
        pltpu.VMEM((width, hidden), BF16),
        pltpu.VMEM((width, hidden), BF16),
        pltpu.VMEM((1, hidden), F32),
        pltpu.VMEM((blocks, tile, hidden), BF16),
        pltpu.VMEM((blocks, slots, tile, tile), jnp.int32),
        pltpu.VMEM((blocks, slots, tile, tile), BF16),
        pltpu.VMEM((blocks, slots, tile, tile), BF16),
        pltpu.VMEM((blocks,) + block, F32),
        pltpu.VMEM((blocks, tile, hidden), F32),
        pltpu.VMEM((blocks,) + block, F32),
        pltpu.VMEM((blocks,) + block, BF16),
        pltpu.VMEM((blocks, tile, hidden), BF16),
        pltpu.VMEM((blocks,) + block, BF16),
        pltpu.VMEM((blocks, tile, hidden), BF16),
        pltpu.VMEM((blocks,) + block, F32),
        pltpu.VMEM((turns * panel,) + block, BF16),
        pltpu.VMEM((turns * panel,) + block, BF16),
        pltpu.VMEM((turns * panel,) + block, BF16),
        pltpu.VMEM((turns * panel,) + block, BF16),
        pltpu.VMEM((tiles + 1,) + block, F32),
        pltpu.VMEM((tiles + 1,) + block, F32),
        pltpu.VMEM((turns * panel + 1,) + block, F32),
        pltpu.VMEM((2, part) + block, F32),
        pltpu.VMEM((blocks,) + block, F32),
        pltpu.VMEM((2, part) + block, BF16),
        pltpu.VMEM((2, 2, part) + block, BF16),
        pltpu.VMEM((2, part) + block, BF16),
        pltpu.VMEM((2, 2, part) + block, BF16),
        pltpu.VMEM((8, 128), jnp.int32),
        pltpu.SMEM((8, 128), jnp.int32),
        pltpu.VMEM((reps, width + 8, 128), F32),
        pltpu.VMEM((reps - 1, width + 8, 128), F32),
        pltpu.VMEM((subs, rows_each + 8, 128), F32),
        pltpu.VMEM((subs - 1, rows_each + 8, 128), F32),
        pltpu.VMEM((rows_each + 8, 128), F32),
        pltpu.VMEM((layers - 1, rows_each + 8, 128), F32),
        pltpu.VMEM((subs, rows_each, 128), F32),
        pltpu.VMEM((reps, width, 128), F32),
        dma((5,)), dma((blocks,)), dma, dma((2,)),
        dma((turns,)), dma((turns,)), dma((turns,)), dma((turns,)), dma((6,)), dma((6,)),
        dma((reps - 1,)), dma((reps - 1,)), dma((subs - 1,)), dma((subs - 1,)),
        dma((layers - 1,)), dma((layers - 1,)), dma((subs - 1,)), dma((subs - 1,)),
        dma((reps - 1,)), dma((reps - 1,)),
    ]
    act, gf, gs, gn, gb = pl.pallas_call(
        functools.partial(kernel, sizes),
        out_shape=(
            jax.ShapeDtypeStruct((blocks, tile, hidden), BF16),
            jax.ShapeDtypeStruct((blocks,) + block, F32),
            jax.ShapeDtypeStruct((width, hidden), F32),
            jax.ShapeDtypeStruct((width, hidden), F32),
            jax.ShapeDtypeStruct((1, hidden), F32),
        ),
        in_specs=[any_space] * 6 + [smem] * 2,
        out_specs=(any_space, any_space, vmem, vmem, vmem),
        scratch_shapes=scratch,
        compiler_params=pltpu.CompilerParams(
            collective_id=0, has_side_effects=True, vmem_limit_bytes=48 * 1024 * 1024
        ),
    )(
        features.reshape((part_blocks,) + block),
        w_self,
        w_neigh,
        bias.reshape(1, hidden),
        cotangent.reshape(blocks, tile, hidden),
        tile_masks,
        slot_source,
        panel_blocks,
    )
    return (
        act.reshape(blocks * tile, hidden),
        gf.reshape(blocks * tile, width),
        gs,
        gn,
        gb.reshape(hidden),
    )


def solution(mesh):
    doms, reps = mesh.shape["dom"], mesh.shape["rep"]
    subs = 16 if doms % 16 == 0 else doms // 2
    offsets = (1, -1, 2, -2, 3, -3)
    in_specs = (
        P("dom", None),
        P(),
        P(),
        P(),
        P(("dom", "rep"), None),
        P(("dom", "rep"), None),
        P(("dom", "rep"), None, None, None),
        P("dom", None, None),
    )
    out_specs = (P(("dom", "rep"), None), P(("dom", "rep"), None), P(), P(), P())

    def step(features, *rest):
        nodes = features.shape[0] * doms
        return per_device((doms, reps, subs, offsets, nodes), features, *rest)

    return jax.shard_map(step, mesh=mesh, in_specs=in_specs, out_specs=out_specs, check_vma=False)
```

time: 596 us -> 89.6 us (0.15)
  waiting for transfers between devices: 338 us -> 0 us
  blocking collectives: 110 us -> 0 us
  Pallas kernels: 0 us -> 76.3 us
  starting transfers between devices: 61.3 us -> 0 us
  other arithmetic: 29.2 us -> 0 us
  local copies, waits for them, and re-layouts: 27.4 us -> 11.1 us
  between operations: 16 us -> 0.65 us
  matrix products: 11.7 us -> 0 us
    psum x1 -> x0, waiting for transfers between devices: 338 us -> none  [per_device(): lax.psum((part_self, part_neigh, part_bias), ('dom', 'rep'))]
    psum x1 -> x0, blocking collectives: 110 us -> none  [per_device(): lax.psum((part_self, part_neigh, part_bias), ('dom', 'rep'))]
    pallas_call x0 -> x1, Pallas kernels: none -> 76.3 us  [per_device(): pl.pallas_call(functools.partial(kernel, sizes), out_shape=(jax.ShapeDtyp...]
    ppermute x12 -> x0, starting transfers between devices: 61.2 us -> none  [passed_along(): return lax.ppermute(block, axis, route)]
    scatter-add x7 -> x0, other arithmetic: 15.5 us -> none  [the longest x1 9.08 us: per_device(): src_grad = jnp.zeros((source_count, tile, in_width), jnp.float32).at[slot...]
    gather x7 -> x0, local copies, waits for them, and re-layouts: 13.4 us -> none  [the longest x6 9.88 us: per_device(): outgoing = own_blocks[panel_blocks[0, turn]]]
    dot_general x8 -> x0, matrix products: 11.7 us -> none  [the longest x1 2.29 us: per_device(): jnp.einsum('dsij,dif->dsjf', mask_w, q_blocks, preferred_element_type=jnp...]
    convert_element_type x9 -> x0, other arithmetic: 6 us -> none  [the longest x6 4.81 us: per_device(): returned = passed_along(panel_grad[turn].astype(jnp.bfloat16), 'dom', -of...]
  transfers between devices with their start and end apart: 14 -> 0, of which waited for: 1 -> 0; matrix products, arithmetic and copies ran while one was open for 6% -> 0% of each run, Pallas kernels for 0% -> 0%
where the time goes in v1:
time: 89.6 us; the launch traced here: 88.1 us
  Pallas kernels  76.3 us (85%)
  local copies, waits for them, and re-layouts  11.1 us (12%)
    pallas_call x1, Pallas kernels, per_device(): pl.pallas_call(functools.partial(kernel, sizes), out_shape=(jax.ShapeDtyp...  76.3 us
    unnamed x20, local copies, waits for them, and re-layouts  11.1 us

profile of v1, /device:TPU:1, one launch (start us, length us, event | category | flops | bytes accessed | tf_op | source)
XLA Modules:
  0.0 88.1 jit_solution(5208215758205626445)
XLA Ops:
  0.6 0.7 copy.13.panel_ref
  1.3 0.0 copy-start
  1.3 1.9 %copy-done = s32[6,8,128,128]{3,2,1,0:T(8,128)S(1)} copy-done((s32[6,8,128,128]{3,2,1,0:T(8,128)S(1)}, s32[6,8,128,128]{3,2,1,0:T(8,128)}, u32[]{:S(2)}) %copy-start) | copy-done | bytes 3145752
  3.2 0.0 copy-start.1
  3.2 1.1 %copy-done.1 = bf16[3072,128]{1,0:T(8,128)(2,1)S(1)} copy-done((bf16[3072,128]{1,0:T(8,128)(2,1)S(1)}, bf16[3072,128]{1,0:T(8,128)(2,1)}, u32[]{:S(2)}) %copy-start.1) | copy-done | bytes 786456
  4.3 0.0 copy-start.2
  4.3 1.0 %copy-done.2 = bf16[768,256]{1,0:T(8,128)(2,1)S(1)} copy-done((bf16[768,256]{1,0:T(8,128)(2,1)S(1)}, bf16[768,256]{1,0:T(8,128)(2,1)}, u32[]{:S(2)}) %copy-start.2) | copy-done | bytes 393240
  5.3 0.0 copy-start.3
  5.3 0.8 copy-done.3
  6.2 0.0 copy-start.4
  6.2 0.8 copy-done.4
  7.0 0.0 copy-start.5
  7.0 0.7 copy-done.5
  7.7 0.0 copy-start.6
  7.7 0.7 copy-done.6
  8.4 76.3 %shard_map.119 = (bf16[6,128,256]{2,1,0:T(8,128)(2,1)S(1)}, f32[6,128,128]{2,1,0:T(8,128)S(1)}, f32[128,256]{1,0:T(8,128)S(1)}, f32[128,256]{1,0:T(8,128)S(1)}, f32[1,256]{1,0:T(1,128)S(1)}) custom-call(bf16[24,128,128]{2,1,0:T(8,128)(2,1)S(1)} %bitcast.6, bf16[128,256]{1,0:T(8,128)(2,1)S(1)} %copy-done.3, bf16[128,256]{1,0:T(8,128)(2,1)S(1)} %copy-done.4, ...), custom_call_target="tpu_custom_call" | custom-call | tf_op jit(solution)/shard_map/pallas_call | solution.py:447
  84.7 0.7 copy.19
  85.5 0.7 copy.20
  86.2 0.7 copy.21
  86.9 0.7 copy.22
  87.5 0.6 copy.23
Async XLA Ops:
  1.3 1.9 %copy-start = (s32[6,8,128,128]{3,2,1,0:T(8,128)S(1)}, s32[6,8,128,128]{3,2,1,0:T(8,128)}, u32[]{:S(2)}) copy-start(s32[6,8,128,128]{3,2,1,0:T(8,128)} %masks_hbm.1) | copy-start | bytes 9437188
  3.2 1.1 %copy-start.1 = (bf16[3072,128]{1,0:T(8,128)(2,1)S(1)}, bf16[3072,128]{1,0:T(8,128)(2,1)}, u32[]{:S(2)}) copy-start(bf16[3072,128]{1,0:T(8,128)(2,1)} %param.8) | copy-start | bytes 2359300
  4.3 1.0 %copy-start.2 = (bf16[768,256]{1,0:T(8,128)(2,1)S(1)}, bf16[768,256]{1,0:T(8,128)(2,1)}, u32[]{:S(2)}) copy-start(bf16[768,256]{1,0:T(8,128)(2,1)} %param.12) | copy-start | bytes 1179652
  5.3 0.8 copy-start.3
  6.2 0.8 copy-start.4
  7.0 0.7 copy-start.5
  7.7 0.7 copy-start.6

commit v2 on v1

--- a/solution.py
+++ b/solution.py
@@ -50,11 +50,18 @@
     half = slots // 2
     part_blocks, tile, width = feat.shape
     hidden = w_self.shape[1]
-    rows_each = width // subs
+    ways = 2 * reps
+    ranks = subs // 2
+    half_rows = width // 2
+    rows_each = half_rows // ranks
     dom = lax.axis_index("dom")
     rep = lax.axis_index("rep")
     layer = dom // subs
     sub = dom % subs
+    rank = sub // 2
+    core = dom % 2
+    other = 1 - 2 * core
+    piece = rep * 2 + core
 
     def received(i, k):
         return jnp.maximum(slot_ref[i, 2 * k + 1] - part_blocks, 0)
@@ -78,25 +85,18 @@
 
     for offset in offsets:
         greet((dom + offset + doms) % doms, rep)
-    for k in range(1, reps):
-        greet(dom, (rep + k) % reps)
-
-    def greet_sub(k, carry):
-        greet(layer * subs + (sub + k) % subs, rep)
-        return carry
-
-    def greet_layer(k, carry):
+    for m in range(1, ways):
+        greet(dom + other * (m // reps), (rep + m) % reps)
+    for k in range(1, ranks):
+        greet(layer * subs + ((rank + k) % ranks) * 2 + core, rep)
+    for k in range(1, layers):
         greet(((layer + k) % layers) * subs + sub, rep)
-        return carry
-
-    lax.fori_loop(1, subs, greet_sub, 0)
-    lax.fori_loop(1, layers, greet_layer, 0)
 
     loads[0].wait()
     for t in range(turns):
         for i in range(panel):
-            panel_out[t * panel + i] = feat[panel_ref[0, t, i]]
-    pl.semaphore_wait(barrier, turns + reps - 1 + subs - 1 + layers - 1)
+            panel_out[t * panel + i] = feat[panel_ref[t, 0, i]]
+    pl.semaphore_wait(barrier, turns + ways - 1 + ranks - 1 + layers - 1)
 
     def to_dom(t, source, target, send, recv_sem, offset):
         part = pl.ds(t * panel, panel)
@@ -111,7 +111,7 @@
 
     odd = [received(i, k) for i in range(blocks) for k in range(half)]
     even = [slot_ref[i, 2 * k] for i in range(blocks) for k in range(half)]
-    back = [panel_ref[0, t, i] for t in range(turns) for i in range(panel)]
+    back = [panel_ref[t, 0, i] for t in range(turns) for i in range(panel)]
     for at, values in enumerate((odd, even, back)):
         prev, last = chain(values)
         idx_v[2 * at : 2 * at + 1, :] = prev
@@ -192,23 +192,67 @@
 
     zero = jnp.zeros((width, hidden), F32)
     part_self, part_neigh = lax.fori_loop(0, blocks, weights, (zero, zero))
+    row = lax.broadcasted_iota(jnp.int32, (bias_rows, 128), 0)
+    bias_tile = jnp.where(row == 0, bias_total[:, :128], jnp.where(row == 1, bias_total[:, 128:], 0.0))
     for at, part in enumerate((part_self, part_neigh)):
         for c in range(2):
-            r1_out[2 * at + c, 0:width] = part[:, c * 128 : (c + 1) * 128]
-    row = lax.broadcasted_iota(jnp.int32, (bias_rows, 128), 0)
-    bias_tile = jnp.where(row == 0, bias_total[:, :128], jnp.where(row == 1, bias_total[:, 128:], 0.0))
-    for at in range(reps):
-        r1_out[at, width : width + bias_rows] = bias_tile
-
-    def stage_1(k):
-        peer = (rep + k) % reps
-        return pltpu.make_async_remote_copy(
-            src_ref=r1_out.at[peer], dst_ref=r1_in.at[k - 1], send_sem=s1_send.at[k - 1], recv_sem=s1_recv.at[k - 1],
-            device_id=(dom, peer), device_id_type=MESH,
-        )
-
-    for k in range(1, reps):
-        stage_1(k).start()
+            for h in range(2):
+                to = (2 * at + c) * 2 + h
+                r1_out[to, 0:half_rows] = part[h * half_rows : (h + 1) * half_rows, c * 128 : (c + 1) * 128]
+                r1_out[to, half_rows : half_rows + bias_rows] = bias_tile
+
+    def near_by(m):
+        return dom + other * (m // reps), (rep + m) % reps
+
+    def stage_1(m):
+        peer, peer_rep = near_by(m)
+        return pltpu.make_async_remote_copy(
+            src_ref=r1_out.at[peer_rep * 2 + peer % 2], dst_ref=r1_in.at[m - 1],
+            send_sem=s1_send.at[m - 1], recv_sem=s1_recv.at[m - 1],
+            device_id=(peer, peer_rep), device_id_type=MESH,
+        )
+
+    def stage_2(k):
+        peer = (rank + k) % ranks
+        return pltpu.make_async_remote_copy(
+            src_ref=r2_out.at[peer], dst_ref=r2_in.at[k - 1], send_sem=s2_send.at[k - 1], recv_sem=s2_recv.at[k - 1],
+            device_id=(layer * subs + peer * 2 + core, rep), device_id_type=MESH,
+        )
+
+    def stage_3(k):
+        peer = (layer + k) % layers
+        return pltpu.make_async_remote_copy(
+            src_ref=r3_out, dst_ref=r3_in.at[k - 1], send_sem=s3_send.at[k - 1], recv_sem=s3_recv.at[k - 1],
+            device_id=(peer * subs + sub, rep), device_id_type=MESH,
+        )
+
+    def stage_4(k):
+        peer = (rank + k) % ranks
+        return pltpu.make_async_remote_copy(
+            src_ref=r4.at[rank], dst_ref=r4.at[rank], send_sem=s4_send.at[k - 1], recv_sem=s4_recv.at[k - 1],
+            device_id=(layer * subs + peer * 2 + core, rep), device_id_type=MESH,
+        )
+
+    def stage_5(m):
+        peer, peer_rep = near_by(m)
+        return pltpu.make_async_remote_copy(
+            src_ref=r5.at[piece], dst_ref=r5.at[piece], send_sem=s5_send.at[m - 1], recv_sem=s5_recv.at[m - 1],
+            device_id=(peer, peer_rep), device_id_type=MESH,
+        )
+
+    def start_all(stage, count):
+        for k in range(1, count):
+            stage(k).start()
+
+    def receive_all(stage, count):
+        for k in range(1, count):
+            stage(k).wait_recv()
+
+    def finish_all(stage, count):
+        for k in range(1, count):
+            stage(k).wait_send()
+
+    start_all(stage_1, ways)
 
     def backward(i, carry):
         q = q_b[i]
@@ -220,68 +264,17 @@
 
     lax.fori_loop(0, blocks, backward, 0)
 
-    for k in range(1, reps):
-        stage_1(k).wait_recv()
-    summed = r1_out[rep]
-    for k in range(1, reps):
-        summed = summed + r1_in[k - 1]
-    for j in range(subs):
+    receive_all(stage_1, ways)
+    summed = r1_out[piece]
+    for m in range(1, ways):
+        summed = summed + r1_in[m - 1]
+    for j in range(ranks):
         r2_out[j, 0:rows_each] = summed[j * rows_each : (j + 1) * rows_each]
-        r2_out[j, rows_each : rows_each + bias_rows] = summed[width : width + bias_rows]
-
-    def stage_2(k):
-        peer = (sub + k) % subs
-        return pltpu.make_async_remote_copy(
-            src_ref=r2_out.at[peer], dst_ref=r2_in.at[k - 1], send_sem=s2_send.at[k - 1], recv_sem=s2_recv.at[k - 1],
-            device_id=(layer * subs + peer, rep), device_id_type=MESH,
-        )
-
-    def stage_3(k):
-        peer = (layer + k) % layers
-        return pltpu.make_async_remote_copy(
-            src_ref=r3_out, dst_ref=r3_in.at[k - 1], send_sem=s3_send.at[k - 1], recv_sem=s3_recv.at[k - 1],
-            device_id=(peer * subs + sub, rep), device_id_type=MESH,
-        )
-
-    def stage_4(k):
-        peer = (sub + k) % subs
-        return pltpu.make_async_remote_copy(
-            src_ref=r4.at[sub], dst_ref=r4.at[sub], send_sem=s4_send.at[k - 1], recv_sem=s4_recv.at[k - 1],
-            device_id=(layer * subs + peer, rep), device_id_type=MESH,
-        )
-
-    def stage_5(k):
-        peer = (rep + k) % reps
-        return pltpu.make_async_remote_copy(
-            src_ref=r5.at[rep], dst_ref=r5.at[rep], send_sem=s5_send.at[k - 1], recv_sem=s5_recv.at[k - 1],
-            device_id=(dom, peer), device_id_type=MESH,
-        )
-
-    def start_all(stage, count):
-        def step(k, carry):
-            stage(k).start()
-            return carry
-
-        lax.fori_loop(1, count, step, 0)
-
-    def receive_all(stage, count):
-        def step(k, carry):
-            stage(k).wait_recv()
-            return carry
-
-        lax.fori_loop(1, count, step, 0)
-
-    def finish_all(stage, count):
-        def step(k, carry):
-            stage(k).wait_send()
-            return carry
-
-        lax.fori_loop(1, count, step, 0)
-
-    start_all(stage_2, subs)
-    receive_all(stage_2, subs)
-    summed = r2_out[sub]
-    for k in range(1, subs):
+        r2_out[j, rows_each : rows_each + bias_rows] = summed[half_rows : half_rows + bias_rows]
+    start_all(stage_2, ranks)
+    receive_all(stage_2, ranks)
+    summed = r2_out[rank]
+    for k in range(1, ranks):
         summed = summed + r2_in[k - 1]
     r3_out[...] = summed
     start_all(stage_3, layers)
@@ -299,9 +292,9 @@
     summed = r3_out[...]
     for k in range(1, layers):
         summed = summed + r3_in[k - 1]
-    r4[sub] = summed[0:rows_each]
+    r4[rank] = summed[0:rows_each]
     final_bias = summed[rows_each : rows_each + bias_rows]
-    start_all(stage_4, subs)
+    start_all(stage_4, ranks)
     for t in order[turns // 2 :]:
         take(t)
 
@@ -343,11 +336,9 @@
     for j in range(blocks):
         own_mine[j] = owned(rep * blocks + j) + gf[j]
 
-    receive_all(stage_4, subs)
-    for j in range(subs):
-        r5[rep, j * rows_each : (j + 1) * rows_each] = r4[j]
-    for k in range(1, reps):
-        stage_5(k).start()
+    receive_all(stage_4, ranks)
+    r5[piece] = r4[...].reshape(half_rows, 128).astype(BF16)
+    start_all(stage_5, ways)
 
     for s in range(2):
         near[s][0].wait_recv()
@@ -361,12 +352,14 @@
     gf_copy.start()
 
     scale = 1.0 / math.sqrt(nodes)
-    for k in range(1, reps):
-        stage_5(k).wait_recv()
+    receive_all(stage_5, ways)
     for c in range(2):
-        gs_ref[:, c * 128 : (c + 1) * 128] = r5[c] * scale
-        gn_ref[:, c * 128 : (c + 1) * 128] = r5[2 + c] * scale
-        gb_ref[:, c * 128 : (c + 1) * 128] = final_bias[c : c + 1] * scale
+        columns = slice(c * 128, (c + 1) * 128)
+        for h in range(2):
+            rows = slice(h * half_rows, (h + 1) * half_rows)
+            gs_ref[rows, columns] = r5[c * 2 + h].astype(F32) * scale
+            gn_ref[rows, columns] = r5[(2 + c) * 2 + h].astype(F32) * scale
+        gb_ref[:, columns] = final_bias[c : c + 1] * scale
 
     for send in sends + returns:
         send.wait_send()
@@ -374,13 +367,27 @@
         passing[s].wait_send()
         for h in range(2):
             near[s][h].wait_send()
-    finish_all(stage_1, reps)
-    finish_all(stage_2, subs)
+    finish_all(stage_1, ways)
+    finish_all(stage_2, ranks)
     finish_all(stage_3, layers)
-    finish_all(stage_4, subs)
-    finish_all(stage_5, reps)
+    finish_all(stage_4, ranks)
+    finish_all(stage_5, ways)
     act_copy.wait()
     gf_copy.wait()
+
+
+def write_out(*refs):
+    count = (len(refs) - 1) // 3
+    given, results, held, sem = refs[:count], refs[count : 2 * count], refs[2 * count : 3 * count], refs[-1]
+    reads = [pltpu.make_async_copy(given[i], held[i], sem.at[0, i]) for i in range(count)]
+    writes = [pltpu.make_async_copy(held[i], results[i], sem.at[1, i]) for i in range(count)]
+    for read in reads:
+        read.start()
+    for read, write in zip(reads, writes):
+        read.wait()
+        write.start()
+    for write in writes:
+        write.wait()
 
 
 def per_device(sizes, features, w_self, w_neigh, bias, cotangent, slot_source, tile_masks, panel_blocks):
@@ -391,7 +398,8 @@
     part_blocks = features.shape[0] // tile
     turns, panel = panel_blocks.shape[1:]
     tiles = blocks * slots // 2
-    rows_each = width // subs
+    ways, ranks, half_rows = 2 * reps, subs // 2, width // 2
+    rows_each = half_rows // ranks
     part = blocks // 2
     dma = pltpu.SemaphoreType.DMA
     any_space = pl.BlockSpec(memory_space=pl.ANY)
@@ -430,21 +438,21 @@
         pltpu.VMEM((2, 2, part) + block, BF16),
         pltpu.VMEM((8, 128), jnp.int32),
         pltpu.SMEM((8, 128), jnp.int32),
-        pltpu.VMEM((reps, width + 8, 128), F32),
-        pltpu.VMEM((reps - 1, width + 8, 128), F32),
-        pltpu.VMEM((subs, rows_each + 8, 128), F32),
-        pltpu.VMEM((subs - 1, rows_each + 8, 128), F32),
+        pltpu.VMEM((ways, half_rows + 8, 128), F32),
+        pltpu.VMEM((ways - 1, half_rows + 8, 128), F32),
+        pltpu.VMEM((ranks, rows_each + 8, 128), F32),
+        pltpu.VMEM((ranks - 1, rows_each + 8, 128), F32),
         pltpu.VMEM((rows_each + 8, 128), F32),
         pltpu.VMEM((layers - 1, rows_each + 8, 128), F32),
-        pltpu.VMEM((subs, rows_each, 128), F32),
-        pltpu.VMEM((reps, width, 128), F32),
+        pltpu.VMEM((ranks, rows_each, 128), F32),
+        pltpu.VMEM((ways, half_rows, 128), BF16),
         dma((5,)), dma((blocks,)), dma, dma((2,)),
         dma((turns,)), dma((turns,)), dma((turns,)), dma((turns,)), dma((6,)), dma((6,)),
-        dma((reps - 1,)), dma((reps - 1,)), dma((subs - 1,)), dma((subs - 1,)),
-        dma((layers - 1,)), dma((layers - 1,)), dma((subs - 1,)), dma((subs - 1,)),
-        dma((reps - 1,)), dma((reps - 1,)),
+        dma((ways - 1,)), dma((ways - 1,)), dma((ranks - 1,)), dma((ranks - 1,)),
+        dma((layers - 1,)), dma((layers - 1,)), dma((ranks - 1,)), dma((ranks - 1,)),
+        dma((ways - 1,)), dma((ways - 1,)),
     ]
-    act, gf, gs, gn, gb = pl.pallas_call(
+    results = pl.pallas_call(
         functools.partial(kernel, sizes),
         out_shape=(
             jax.ShapeDtypeStruct((blocks, tile, hidden), BF16),
@@ -457,7 +465,7 @@
         out_specs=(any_space, any_space, vmem, vmem, vmem),
         scratch_shapes=scratch,
         compiler_params=pltpu.CompilerParams(
-            collective_id=0, has_side_effects=True, vmem_limit_bytes=48 * 1024 * 1024
+            collective_id=0, has_side_effects=True, vmem_limit_bytes=63 * 1024 * 1024
         ),
     )(
         features.reshape((part_blocks,) + block),
@@ -467,8 +475,16 @@
         cotangent.reshape(blocks, tile, hidden),
         tile_masks,
         slot_source,
-        panel_blocks,
+        panel_blocks.transpose(1, 0, 2),
     )
+    act, gf, gs, gn, gb = pl.pallas_call(
+        write_out,
+        out_shape=tuple(jax.ShapeDtypeStruct(x.shape, x.dtype) for x in results),
+        in_specs=[any_space] * len(results),
+        out_specs=(any_space,) * len(results),
+        scratch_shapes=[pltpu.VMEM(x.shape, x.dtype) for x in results] + [dma((2, len(results)))],
+        compiler_params=pltpu.CompilerParams(vmem_limit_bytes=63 * 1024 * 1024),
+    )(*results)
     return (
         act.reshape(blocks * tile, hidden),
         gf.reshape(blocks * tile, width),

time: 89.6 us -> 77.7 us (0.87); the launches traced: 88.1 us -> 77.5 us
  local copies, waits for them, and re-layouts: 11.1 us -> 0 us
    unnamed x20 -> x0, local copies, waits for them, and re-layouts: 11.1 us -> none
    pallas_call x0 -> x1, Pallas kernels: none -> 2.04 us  [per_device(): pl.pallas_call(write_out, out_shape=tuple((jax.ShapeDtypeStruct(x.shape,...]
    pallas_call x1, Pallas kernels: 76.3 us -> 74.8 us  [per_device(): pl.pallas_call(functools.partial(kernel, sizes), out_shape=(jax.ShapeDtyp...]
where the time goes in v2:
time: 77.7 us; the launch traced here: 77.5 us
  Pallas kernels  76.8 us (99%)
    pallas_call x1, Pallas kernels, per_device(): pl.pallas_call(functools.partial(kernel, sizes), out_shape=(jax.ShapeDtyp...  74.8 us
    pallas_call x1, Pallas kernels, per_device(): pl.pallas_call(write_out, out_shape=tuple((jax.ShapeDtypeStruct(x.shape,...  2.04 us

profile of v2, /device:TPU:1, one launch (start us, length us, event | category | flops | bytes accessed | tf_op | source)
XLA Modules:
  0.0 77.5 jit_solution(1772785623592886681)
XLA Ops:
  0.6 74.8 %shard_map.119 = (bf16[6,128,256]{2,1,0:T(8,128)(2,1)}, f32[6,128,128]{2,1,0:T(8,128)}, f32[128,256]{1,0:T(8,128)}, f32[128,256]{1,0:T(8,128)}, f32[1,256]{1,0:T(1,128)}) custom-call(bf16[24,128,128]{2,1,0:T(8,128)(2,1)} %bitcast.7, bf16[128,256]{1,0:T(8,128)(2,1)} %w_self_hbm.1, bf16[128,256]{1,0:T(8,128)(2,1)} %w_neigh_hbm.1, f32[1,256]{1,0:T(1,128)} %bitcast.10, ...), custom_call_target="tpu_custom_call" | custom-call | tf_op jit(solution)/shard_map/pallas_call | solution.py:455
  75.4 2.0 %shard_map.120 = (bf16[6,128,256]{2,1,0:T(8,128)(2,1)}, f32[6,128,128]{2,1,0:T(8,128)}, f32[128,256]{1,0:T(8,128)}, f32[128,256]{1,0:T(8,128)}, f32[1,256]{1,0:T(1,128)}) custom-call(bf16[6,128,256]{2,1,0:T(8,128)(2,1)} %get-tuple-element.15.refs_0_, f32[6,128,128]{2,1,0:T(8,128)} %get-tuple-element.16.refs_1_, f32[128,256]{1,0:T(8,128)} %get-tuple-element.17.refs_2_, ...), custom_call_target="tpu_custom_call" | custom-call | tf_op jit(solution)/shard_map/pallas_call | solution.py:480

commit v3 on v2

--- a/solution.py
+++ b/solution.py
@@ -8,6 +8,8 @@
 from jax.experimental.pallas import tpu as pltpu
 from jax.sharding import PartitionSpec as P
 
+LATE = (4, 5)
+UNROLL = 2
 MESH = pl.DeviceIdType.MESH
 F32 = jnp.float32
 BF16 = jnp.bfloat16
@@ -35,11 +37,11 @@
 def kernel(
     sizes, feat_hbm, w_self_hbm, w_neigh_hbm, bias_hbm, cot_hbm, masks_hbm, slot_ref, panel_ref,
     act_hbm, gf_hbm, gs_ref, gn_ref, gb_ref,
-    feat, w_self, w_neigh, bias, cot, masks, mask_b, mask_t, inv, z0, agg_even, agg_b, dz_b, q_b, act, gf,
+    feat, w_self, w_neigh, bias, cot, masks, mask_b, mask_t, inv, z0, agg_even, feat_t, agg_t, dz_b, q_b, act, gf,
     panel_out, recv, grad_out, returned, chain_odd, chain_even, chain_back, own, own_mine, x_pass, x_near,
     got_pass, got_near, idx_v, idx_s,
     r1_out, r1_in, r2_out, r2_in, r3_out, r3_in, r4, r5,
-    in_sem, mask_sem, idx_sem, out_sem, fwd_send, fwd_recv, back_send, back_recv, x_send, x_recv,
+    in_sem, mask_sem, idx_sem, out_sem, fwd_send, fwd_recv, far_send, far_recv, hand_send, hand_recv, back_send, back_recv, x_send, x_recv,
     s1_send, s1_recv, s2_send, s2_recv, s3_send, s3_recv, s4_send, s4_recv, s5_send, s5_recv,
 ):
     doms, reps, subs, offsets, nodes = sizes
@@ -66,6 +68,9 @@
     def received(i, k):
         return jnp.maximum(slot_ref[i, 2 * k + 1] - part_blocks, 0)
 
+    def columns_of(i):
+        return pl.ds(pl.multiple_of(i * tile, tile), tile)
+
     loads = [
         pltpu.make_async_copy(feat_hbm, feat, in_sem.at[0]),
         pltpu.make_async_copy(w_self_hbm, w_self, in_sem.at[1]),
@@ -98,17 +103,39 @@
             panel_out[t * panel + i] = feat[panel_ref[t, 0, i]]
     pl.semaphore_wait(barrier, turns + ways - 1 + ranks - 1 + layers - 1)
 
-    def to_dom(t, source, target, send, recv_sem, offset):
-        part = pl.ds(t * panel, panel)
+    def to_dom(t, source, target, send, recv_sem, offset, count=panel):
+        part = pl.ds(t * panel, count)
         return pltpu.make_async_remote_copy(
             src_ref=source.at[part], dst_ref=target.at[part], send_sem=send.at[t], recv_sem=recv_sem.at[t],
             device_id=((dom + offset + doms) % doms, rep), device_id_type=MESH,
         )
 
-    sends = [to_dom(t, panel_out, recv, fwd_send, fwd_recv, offsets[t]) for t in range(turns)]
+    far = [t for t in range(turns) if abs(offsets[t]) == 3]
+    common = panel - reps
+
+    def to_far(n, source, target, send, recv_sem, way):
+        mine = far[n] * panel + common + rep
+        return pltpu.make_async_remote_copy(
+            src_ref=source.at[mine], dst_ref=target.at[mine], send_sem=send.at[n], recv_sem=recv_sem.at[n],
+            device_id=((dom + way * offsets[far[n]] + doms) % doms, rep), device_id_type=MESH,
+        )
+
+    def hand_on(n, k):
+        mine = far[n] * panel + common + rep
+        at = n * (reps - 1) + k - 1
+        return pltpu.make_async_remote_copy(
+            src_ref=recv.at[mine], dst_ref=recv.at[mine], send_sem=hand_send.at[at], recv_sem=hand_recv.at[at],
+            device_id=(dom, (rep + k) % reps), device_id_type=MESH,
+        )
+
+    shared = [to_far(n, panel_out, recv, far_send, far_recv, 1) for n in range(len(far))]
+    sends = [
+        to_dom(t, panel_out, recv, fwd_send, fwd_recv, offsets[t], common if t in far else panel) for t in range(turns)
+    ]
+    for send in shared:
+        send.start()
     for t in reversed(range(turns)):
         sends[t].start()
-
     odd = [received(i, k) for i in range(blocks) for k in range(half)]
     even = [slot_ref[i, 2 * k] for i in range(blocks) for k in range(half)]
     back = [panel_ref[t, 0, i] for t in range(turns) for i in range(panel)]
@@ -122,6 +149,11 @@
     chain_odd[0] = jnp.zeros((tile, width), F32)
     chain_even[0] = jnp.zeros((tile, width), F32)
     chain_back[0] = jnp.zeros((tile, width), F32)
+    for n in range(len(far)):
+        shared[n].wait_recv()
+        for k in range(1, reps):
+            hand_on(n, k).start()
+
     loads[1].wait()
     loads[2].wait()
     loads[3].wait()
@@ -141,21 +173,26 @@
         agg_even[i] = aggregate
         degree = jnp.maximum(jnp.sum(total, axis=1, keepdims=True), 1.0)
         inv[i] = jnp.broadcast_to(1.0 / degree, (tile, width))
-        z0[i] = dot(feat[rep * blocks + i], w_self[...]) + bias[...]
+        mine = feat[rep * blocks + i]
+        feat_t[:, columns_of(i)] = mine.T
+        z0[i] = dot(mine, w_self[...]) + bias[...]
         return carry
 
-    lax.fori_loop(0, blocks, prepare, 0)
+    lax.fori_loop(0, blocks, prepare, 0, unroll=UNROLL)
     loads[4].wait()
     idx_copy.wait()
     for send in sends:
         send.wait_recv()
+    for n in range(len(far)):
+        for k in range(1, reps):
+            hand_on(n, k).wait_recv()
 
     def forward(i, bias_total):
         aggregate = agg_even[i]
         for k in range(half):
             aggregate = aggregate + dot(mask_b[i, 2 * k + 1], recv[received(i, k)])
         agg = (aggregate * inv[i]).astype(BF16)
-        agg_b[i] = agg
+        agg_t[:, columns_of(i)] = agg.T
         z = z0[i] + dot(agg, w_neigh[...])
         sig = lax.logistic(z)
         act[i] = (z * sig).astype(BF16)
@@ -165,94 +202,98 @@
         q = lax.dot_general(dzb, w_neigh[...], CONTRACT_LANES, preferred_element_type=F32)
         q = (q * inv[i]).astype(BF16)
         q_b[i] = q
+        return bias_total + jnp.sum(dz, axis=0, keepdims=True)
+
+    bias_total = lax.fori_loop(0, blocks, forward, jnp.zeros((1, hidden), F32), unroll=UNROLL)
+    act_copy = pltpu.make_async_copy(act, act_hbm, out_sem.at[0])
+    act_copy.start()
+
+    bias_rows = 8
+    packed_rows = 16
+    dz_all = dz_b[...].reshape(blocks * tile, hidden)
+    row = lax.broadcasted_iota(jnp.int32, (packed_rows, 128), 0)
+    bias_high = bias_total.astype(BF16).astype(F32)
+    bias_low = bias_total - bias_high
+    bias_tile = jnp.zeros((packed_rows, 128), F32)
+    for at, line in enumerate((bias_high, bias_low)):
+        for c in range(2):
+            bias_tile = jnp.where(row == 2 * at + c, line[:, c * 128 : (c + 1) * 128], bias_tile)
+    bias_tile = bias_tile.astype(BF16)
+    for at, left_side in enumerate((feat_t, agg_t)):
+        part = dot(left_side[...], dz_all).astype(BF16)
+        for c in range(2):
+            for h in range(2):
+                to = (2 * at + c) * 2 + h
+                r1_out[to, 0:half_rows] = part[h * half_rows : (h + 1) * half_rows, c * 128 : (c + 1) * 128]
+                r1_out[to, half_rows : half_rows + packed_rows] = bias_tile
+
+    def near_by(m):
+        return dom + other * (m // reps), (rep + m) % reps
+
+    def stage_1(m):
+        peer, peer_rep = near_by(m)
+        return pltpu.make_async_remote_copy(
+            src_ref=r1_out.at[peer_rep * 2 + peer % 2], dst_ref=r1_in.at[m - 1],
+            send_sem=s1_send.at[m - 1], recv_sem=s1_recv.at[m - 1],
+            device_id=(peer, peer_rep), device_id_type=MESH,
+        )
+
+    def stage_2(k):
+        peer = (rank + k) % ranks
+        return pltpu.make_async_remote_copy(
+            src_ref=r2_out.at[peer], dst_ref=r2_in.at[k - 1], send_sem=s2_send.at[k - 1], recv_sem=s2_recv.at[k - 1],
+            device_id=(layer * subs + peer * 2 + core, rep), device_id_type=MESH,
+        )
+
+    def stage_3(k):
+        peer = (layer + k) % layers
+        return pltpu.make_async_remote_copy(
+            src_ref=r3_out, dst_ref=r3_in.at[k - 1], send_sem=s3_send.at[k - 1], recv_sem=s3_recv.at[k - 1],
+            device_id=(peer * subs + sub, rep), device_id_type=MESH,
+        )
+
+    def stage_4(k):
+        peer = (rank + k) % ranks
+        return pltpu.make_async_remote_copy(
+            src_ref=r4.at[rank], dst_ref=r4.at[rank], send_sem=s4_send.at[k - 1], recv_sem=s4_recv.at[k - 1],
+            device_id=(layer * subs + peer * 2 + core, rep), device_id_type=MESH,
+        )
+
+    def stage_5(m):
+        peer, peer_rep = near_by(m)
+        return pltpu.make_async_remote_copy(
+            src_ref=r5.at[piece], dst_ref=r5.at[piece], send_sem=s5_send.at[m - 1], recv_sem=s5_recv.at[m - 1],
+            device_id=(peer, peer_rep), device_id_type=MESH,
+        )
+
+    def start_all(stage, count):
+        for k in range(1, count):
+            stage(k).start()
+
+    def receive_all(stage, count):
+        for k in range(1, count):
+            stage(k).wait_recv()
+
+    def finish_all(stage, count):
+        for k in range(1, count):
+            stage(k).wait_send()
+
+    start_all(stage_1, ways)
+
+    def backward_received(i, carry):
+        q = q_b[i]
         for k in range(half):
             at = i * half + k
             chain_odd[at + 1] = chain_odd[idx_s[0, at]] + dot(mask_t[i, 2 * k + 1], q)
-        return bias_total + jnp.sum(dz, axis=0, keepdims=True)
-
-    bias_total = lax.fori_loop(0, blocks, forward, jnp.zeros((1, hidden), F32))
-    act_copy = pltpu.make_async_copy(act, act_hbm, out_sem.at[0])
-    act_copy.start()
+        return carry
+
+    lax.fori_loop(0, blocks, backward_received, 0, unroll=UNROLL)
     returns = [to_dom(t, grad_out, returned, back_send, back_recv, -offsets[t]) for t in range(turns)]
     for t in reversed(range(turns)):
         for i in range(panel):
             grad_out[t * panel + i] = chain_odd[idx_s[1, t * panel + i]].astype(BF16)
-        returns[t].start()
-
-    bias_rows = 8
-
-    def weights(i, carry):
-        part_self, part_neigh = carry
-        dzb = dz_b[i]
-        part_self = part_self + lax.dot_general(
-            feat[rep * blocks + i], dzb, CONTRACT_ROWS, preferred_element_type=F32
-        )
-        part_neigh = part_neigh + lax.dot_general(agg_b[i], dzb, CONTRACT_ROWS, preferred_element_type=F32)
-        return part_self, part_neigh
-
-    zero = jnp.zeros((width, hidden), F32)
-    part_self, part_neigh = lax.fori_loop(0, blocks, weights, (zero, zero))
-    row = lax.broadcasted_iota(jnp.int32, (bias_rows, 128), 0)
-    bias_tile = jnp.where(row == 0, bias_total[:, :128], jnp.where(row == 1, bias_total[:, 128:], 0.0))
-    for at, part in enumerate((part_self, part_neigh)):
-        for c in range(2):
-            for h in range(2):
-                to = (2 * at + c) * 2 + h
-                r1_out[to, 0:half_rows] = part[h * half_rows : (h + 1) * half_rows, c * 128 : (c + 1) * 128]
-                r1_out[to, half_rows : half_rows + bias_rows] = bias_tile
-
-    def near_by(m):
-        return dom + other * (m // reps), (rep + m) % reps
-
-    def stage_1(m):
-        peer, peer_rep = near_by(m)
-        return pltpu.make_async_remote_copy(
-            src_ref=r1_out.at[peer_rep * 2 + peer % 2], dst_ref=r1_in.at[m - 1],
-            send_sem=s1_send.at[m - 1], recv_sem=s1_recv.at[m - 1],
-            device_id=(peer, peer_rep), device_id_type=MESH,
-        )
-
-    def stage_2(k):
-        peer = (rank + k) % ranks
-        return pltpu.make_async_remote_copy(
-            src_ref=r2_out.at[peer], dst_ref=r2_in.at[k - 1], send_sem=s2_send.at[k - 1], recv_sem=s2_recv.at[k - 1],
-            device_id=(layer * subs + peer * 2 + core, rep), device_id_type=MESH,
-        )
-
-    def stage_3(k):
-        peer = (layer + k) % layers
-        return pltpu.make_async_remote_copy(
-            src_ref=r3_out, dst_ref=r3_in.at[k - 1], send_sem=s3_send.at[k - 1], recv_sem=s3_recv.at[k - 1],
-            device_id=(peer * subs + sub, rep), device_id_type=MESH,
-        )
-
-    def stage_4(k):
-        peer = (rank + k) % ranks
-        return pltpu.make_async_remote_copy(
-            src_ref=r4.at[rank], dst_ref=r4.at[rank], send_sem=s4_send.at[k - 1], recv_sem=s4_recv.at[k - 1],
-            device_id=(layer * subs + peer * 2 + core, rep), device_id_type=MESH,
-        )
-
-    def stage_5(m):
-        peer, peer_rep = near_by(m)
-        return pltpu.make_async_remote_copy(
-            src_ref=r5.at[piece], dst_ref=r5.at[piece], send_sem=s5_send.at[m - 1], recv_sem=s5_recv.at[m - 1],
-            device_id=(peer, peer_rep), device_id_type=MESH,
-        )
-
-    def start_all(stage, count):
-        for k in range(1, count):
-            stage(k).start()
-
-    def receive_all(stage, count):
-        for k in range(1, count):
-            stage(k).wait_recv()
-
-    def finish_all(stage, count):
-        for k in range(1, count):
-            stage(k).wait_send()
-
-    start_all(stage_1, ways)
+        if t not in LATE:
+            returns[t].start()
 
     def backward(i, carry):
         q = q_b[i]
@@ -265,13 +306,16 @@
     lax.fori_loop(0, blocks, backward, 0)
 
     receive_all(stage_1, ways)
-    summed = r1_out[piece]
+    summed = r1_out[piece].astype(F32)
     for m in range(1, ways):
-        summed = summed + r1_in[m - 1]
+        summed = summed + r1_in[m - 1].astype(F32)
+    bias_high = summed[half_rows : half_rows + bias_rows]
     for j in range(ranks):
         r2_out[j, 0:rows_each] = summed[j * rows_each : (j + 1) * rows_each]
-        r2_out[j, rows_each : rows_each + bias_rows] = summed[half_rows : half_rows + bias_rows]
+        r2_out[j, rows_each : rows_each + bias_rows] = bias_high
     start_all(stage_2, ranks)
+    for t in LATE:
+        returns[t].start()
     receive_all(stage_2, ranks)
     summed = r2_out[rank]
     for k in range(1, ranks):
@@ -286,7 +330,7 @@
             chain_back[at + 1] = chain_back[idx_s[4, at]] + returned[at].astype(F32)
 
     order = list(range(turns))
-    for t in order[: turns // 2]:
+    for t in order[:4]:
         take(t)
     receive_all(stage_3, layers)
     summed = r3_out[...]
@@ -295,7 +339,7 @@
     r4[rank] = summed[0:rows_each]
     final_bias = summed[rows_each : rows_each + bias_rows]
     start_all(stage_4, ranks)
-    for t in order[turns // 2 :]:
+    for t in order[4:]:
         take(t)
 
     right, left, across = (rep + 1) % reps, (rep + 3) % reps, (rep + 2) % reps
@@ -359,10 +403,13 @@
             rows = slice(h * half_rows, (h + 1) * half_rows)
             gs_ref[rows, columns] = r5[c * 2 + h].astype(F32) * scale
             gn_ref[rows, columns] = r5[(2 + c) * 2 + h].astype(F32) * scale
-        gb_ref[:, columns] = final_bias[c : c + 1] * scale
-
-    for send in sends + returns:
+        gb_ref[:, columns] = (final_bias[c : c + 1] + final_bias[2 + c : 3 + c]) * scale
+
+    for send in shared + sends + returns:
         send.wait_send()
+    for n in range(len(far)):
+        for k in range(1, reps):
+            hand_on(n, k).wait_send()
     for s in range(2):
         passing[s].wait_send()
         for h in range(2):
@@ -418,7 +465,8 @@
         pltpu.VMEM((blocks,) + block, F32),
         pltpu.VMEM((blocks, tile, hidden), F32),
         pltpu.VMEM((blocks,) + block, F32),
-        pltpu.VMEM((blocks,) + block, BF16),
+        pltpu.VMEM((width, blocks * tile), BF16),
+        pltpu.VMEM((width, blocks * tile), BF16),
         pltpu.VMEM((blocks, tile, hidden), BF16),
         pltpu.VMEM((blocks,) + block, BF16),
         pltpu.VMEM((blocks, tile, hidden), BF16),
@@ -438,8 +486,8 @@
         pltpu.VMEM((2, 2, part) + block, BF16),
         pltpu.VMEM((8, 128), jnp.int32),
         pltpu.SMEM((8, 128), jnp.int32),
-        pltpu.VMEM((ways, half_rows + 8, 128), F32),
-        pltpu.VMEM((ways - 1, half_rows + 8, 128), F32),
+        pltpu.VMEM((ways, half_rows + 16, 128), BF16),
+        pltpu.VMEM((ways - 1, half_rows + 16, 128), BF16),
         pltpu.VMEM((ranks, rows_each + 8, 128), F32),
         pltpu.VMEM((ranks - 1, rows_each + 8, 128), F32),
         pltpu.VMEM((rows_each + 8, 128), F32),
@@ -447,7 +495,8 @@
         pltpu.VMEM((ranks, rows_each, 128), F32),
         pltpu.VMEM((ways, half_rows, 128), BF16),
         dma((5,)), dma((blocks,)), dma, dma((2,)),
-        dma((turns,)), dma((turns,)), dma((turns,)), dma((turns,)), dma((6,)), dma((6,)),
+        dma((turns,)), dma((turns,)), dma((2,)), dma((2,)), dma((2 * reps - 2,)), dma((2 * reps - 2,)),
+        dma((turns,)), dma((turns,)), dma((6,)), dma((6,)),
         dma((ways - 1,)), dma((ways - 1,)), dma((ranks - 1,)), dma((ranks - 1,)),
         dma((layers - 1,)), dma((layers - 1,)), dma((ranks - 1,)), dma((ranks - 1,)),
         dma((ways - 1,)), dma((ways - 1,)),

time: 77.7 us -> 72.8 us (0.937)
  Pallas kernels: 76.8 us -> 72 us
    pallas_call x1, Pallas kernels: 74.8 us -> 69.9 us  [per_device(): pl.pallas_call(functools.partial(kernel, sizes), out_shape=(jax.ShapeDtyp...]
where the time goes in v3:
time: 72.8 us; the launch traced here: 72.6 us
  Pallas kernels  72 us (99%)
    pallas_call x1, Pallas kernels, per_device(): pl.pallas_call(functools.partial(kernel, sizes), out_shape=(jax.ShapeDtyp...  69.9 us
    pallas_call x1, Pallas kernels, per_device(): pl.pallas_call(write_out, out_shape=tuple((jax.ShapeDtypeStruct(x.shape,...  2.04 us

profile of v3, /device:TPU:1, one launch (start us, length us, event | category | flops | bytes accessed | tf_op | source)
XLA Modules:
  0.0 72.6 jit_solution(6402650096313726044)
XLA Ops:
  0.6 69.9 %shard_map.119 = (bf16[6,128,256]{2,1,0:T(8,128)(2,1)}, f32[6,128,128]{2,1,0:T(8,128)}, f32[128,256]{1,0:T(8,128)}, f32[128,256]{1,0:T(8,128)}, f32[1,256]{1,0:T(1,128)}) custom-call(bf16[24,128,128]{2,1,0:T(8,128)(2,1)} %bitcast.7, bf16[128,256]{1,0:T(8,128)(2,1)} %w_self_hbm.1, bf16[128,256]{1,0:T(8,128)(2,1)} %w_neigh_hbm.1, f32[1,256]{1,0:T(1,128)} %bitcast.10, ...), custom_call_target="tpu_custom_call" | custom-call | tf_op jit(solution)/shard_map/pallas_call | solution.py:504
  70.6 2.0 %shard_map.120 = (bf16[6,128,256]{2,1,0:T(8,128)(2,1)}, f32[6,128,128]{2,1,0:T(8,128)}, f32[128,256]{1,0:T(8,128)}, f32[128,256]{1,0:T(8,128)}, f32[1,256]{1,0:T(1,128)}) custom-call(bf16[6,128,256]{2,1,0:T(8,128)(2,1)} %get-tuple-element.15.refs_0_, f32[6,128,128]{2,1,0:T(8,128)} %get-tuple-element.16.refs_1_, f32[128,256]{1,0:T(8,128)} %get-tuple-element.17.refs_2_, ...), custom_call_target="tpu_custom_call" | custom-call | tf_op jit(solution)/shard_map/pallas_call | solution.py:529

commit v4 on v3

--- a/solution.py
+++ b/solution.py
@@ -38,10 +38,10 @@
     sizes, feat_hbm, w_self_hbm, w_neigh_hbm, bias_hbm, cot_hbm, masks_hbm, slot_ref, panel_ref,
     act_hbm, gf_hbm, gs_ref, gn_ref, gb_ref,
     feat, w_self, w_neigh, bias, cot, masks, mask_b, mask_t, inv, z0, agg_even, feat_t, agg_t, dz_b, q_b, act, gf,
-    panel_out, recv, grad_out, returned, chain_odd, chain_even, chain_back, own, own_mine, x_pass, x_near,
+    far_in, far_out, panel_out, recv, grad_out, returned, chain_odd, chain_even, chain_back, own, own_mine, x_pass, x_near,
     got_pass, got_near, idx_v, idx_s,
     r1_out, r1_in, r2_out, r2_in, r3_out, r3_in, r4, r5,
-    in_sem, mask_sem, idx_sem, out_sem, fwd_send, fwd_recv, far_send, far_recv, hand_send, hand_recv, back_send, back_recv, x_send, x_recv,
+    in_sem, mask_sem, idx_sem, out_sem, fwd_send, fwd_recv, far_send, far_recv, hand_send, hand_recv, gather_send, gather_recv, back_far_send, back_far_recv, back_send, back_recv, x_send, x_recv,
     s1_send, s1_recv, s2_send, s2_recv, s3_send, s3_recv, s4_send, s4_recv, s5_send, s5_recv,
 ):
     doms, reps, subs, offsets, nodes = sizes
@@ -71,6 +71,12 @@
     def columns_of(i):
         return pl.ds(pl.multiple_of(i * tile, tile), tile)
 
+    far = [t for t in range(turns) if abs(offsets[t]) == 3]
+    common = panel - reps
+    for t in far:
+        for i in range(common, panel):
+            returned[t * panel + i] = jnp.zeros((tile, width), BF16)
+
     loads = [
         pltpu.make_async_copy(feat_hbm, feat, in_sem.at[0]),
         pltpu.make_async_copy(w_self_hbm, w_self, in_sem.at[1]),
@@ -109,9 +115,6 @@
             src_ref=source.at[part], dst_ref=target.at[part], send_sem=send.at[t], recv_sem=recv_sem.at[t],
             device_id=((dom + offset + doms) % doms, rep), device_id_type=MESH,
         )
-
-    far = [t for t in range(turns) if abs(offsets[t]) == 3]
-    common = panel - reps
 
     def to_far(n, source, target, send, recv_sem, way):
         mine = far[n] * panel + common + rep
@@ -288,10 +291,32 @@
         return carry
 
     lax.fori_loop(0, blocks, backward_received, 0, unroll=UNROLL)
-    returns = [to_dom(t, grad_out, returned, back_send, back_recv, -offsets[t]) for t in range(turns)]
+    returns = [
+        to_dom(t, grad_out, returned, back_send, back_recv, -offsets[t], common if t in far else panel)
+        for t in range(turns)
+    ]
+
+    def gather_far(n, k):
+        peer = (rep + k) % reps
+        at = n * (reps - 1) + k - 1
+        return pltpu.make_async_remote_copy(
+            src_ref=grad_out.at[far[n] * panel + common + peer], dst_ref=far_in.at[at],
+            send_sem=gather_send.at[at], recv_sem=gather_recv.at[at], device_id=(dom, peer), device_id_type=MESH,
+        )
+
+    def return_far(n):
+        return pltpu.make_async_remote_copy(
+            src_ref=far_out.at[n], dst_ref=returned.at[far[n] * panel + common + rep],
+            send_sem=back_far_send.at[n], recv_sem=back_far_recv.at[n],
+            device_id=((dom - offsets[far[n]] + doms) % doms, rep), device_id_type=MESH,
+        )
+
     for t in reversed(range(turns)):
         for i in range(panel):
             grad_out[t * panel + i] = chain_odd[idx_s[1, t * panel + i]].astype(BF16)
+        if t in far:
+            for k in range(1, reps):
+                gather_far(far.index(t), k).start()
         if t not in LATE:
             returns[t].start()
 
@@ -314,6 +339,13 @@
         r2_out[j, 0:rows_each] = summed[j * rows_each : (j + 1) * rows_each]
         r2_out[j, rows_each : rows_each + bias_rows] = bias_high
     start_all(stage_2, ranks)
+    for n in range(len(far)):
+        total = grad_out[far[n] * panel + common + rep].astype(F32)
+        for k in range(1, reps):
+            gather_far(n, k).wait_recv()
+            total = total + far_in[n * (reps - 1) + k - 1].astype(F32)
+        far_out[n] = total.astype(BF16)
+        return_far(n).start()
     for t in LATE:
         returns[t].start()
     receive_all(stage_2, ranks)
@@ -325,6 +357,8 @@
 
     def take(t):
         returns[t].wait_recv()
+        if t in far:
+            return_far(far.index(t)).wait_recv()
         for i in range(panel):
             at = t * panel + i
             chain_back[at + 1] = chain_back[idx_s[4, at]] + returned[at].astype(F32)
@@ -410,6 +444,8 @@
     for n in range(len(far)):
         for k in range(1, reps):
             hand_on(n, k).wait_send()
+            gather_far(n, k).wait_send()
+        return_far(n).wait_send()
     for s in range(2):
         passing[s].wait_send()
         for h in range(2):
@@ -471,6 +507,8 @@
         pltpu.VMEM((blocks,) + block, BF16),
         pltpu.VMEM((blocks, tile, hidden), BF16),
         pltpu.VMEM((blocks,) + block, F32),
+        pltpu.VMEM((2 * reps - 2,) + block, BF16),
+        pltpu.VMEM((2,) + block, BF16),
         pltpu.VMEM((turns * panel,) + block, BF16),
         pltpu.VMEM((turns * panel,) + block, BF16),
         pltpu.VMEM((turns * panel,) + block, BF16),
@@ -496,6 +534,7 @@
         pltpu.VMEM((ways, half_rows, 128), BF16),
         dma((5,)), dma((blocks,)), dma, dma((2,)),
         dma((turns,)), dma((turns,)), dma((2,)), dma((2,)), dma((2 * reps - 2,)), dma((2 * reps - 2,)),
+        dma((2 * reps - 2,)), dma((2 * reps - 2,)), dma((2,)), dma((2,)),
         dma((turns,)), dma((turns,)), dma((6,)), dma((6,)),
         dma((ways - 1,)), dma((ways - 1,)), dma((ranks - 1,)), dma((ranks - 1,)),
         dma((layers - 1,)), dma((layers - 1,)), dma((ranks - 1,)), dma((ranks - 1,)),

time: 72.8 us -> 69.9 us (0.960)
  Pallas kernels: 72 us -> 69.1 us
    pallas_call x1, Pallas kernels: 69.9 us -> 67.1 us  [per_device(): pl.pallas_call(functools.partial(kernel, sizes), out_shape=(jax.ShapeDtyp...]
where the time goes in v4:
time: 69.9 us; the launch traced here: 69.8 us
  Pallas kernels  69.1 us (99%)
    pallas_call x1, Pallas kernels, per_device(): pl.pallas_call(functools.partial(kernel, sizes), out_shape=(jax.ShapeDtyp...  67.1 us
    pallas_call x1, Pallas kernels, per_device(): pl.pallas_call(write_out, out_shape=tuple((jax.ShapeDtypeStruct(x.shape,...  2.04 us

profile of v4, /device:TPU:1, one launch (start us, length us, event | category | flops | bytes accessed | tf_op | source)
XLA Modules:
  0.0 69.8 jit_solution(8744357856944595702)
XLA Ops:
  0.6 67.1 %shard_map.119 = (bf16[6,128,256]{2,1,0:T(8,128)(2,1)}, f32[6,128,128]{2,1,0:T(8,128)}, f32[128,256]{1,0:T(8,128)}, f32[128,256]{1,0:T(8,128)}, f32[1,256]{1,0:T(1,128)}) custom-call(bf16[24,128,128]{2,1,0:T(8,128)(2,1)} %bitcast.7, bf16[128,256]{1,0:T(8,128)(2,1)} %w_self_hbm.1, bf16[128,256]{1,0:T(8,128)(2,1)} %w_neigh_hbm.1, f32[1,256]{1,0:T(1,128)} %bitcast.10, ...), custom_call_target="tpu_custom_call" | custom-call | tf_op jit(solution)/shard_map/pallas_call | solution.py:543
  67.7 2.0 %shard_map.120 = (bf16[6,128,256]{2,1,0:T(8,128)(2,1)}, f32[6,128,128]{2,1,0:T(8,128)}, f32[128,256]{1,0:T(8,128)}, f32[128,256]{1,0:T(8,128)}, f32[1,256]{1,0:T(1,128)}) custom-call(bf16[6,128,256]{2,1,0:T(8,128)(2,1)} %get-tuple-element.15.refs_0_, f32[6,128,128]{2,1,0:T(8,128)} %get-tuple-element.16.refs_1_, f32[128,256]{1,0:T(8,128)} %get-tuple-element.17.refs_2_, ...), custom_call_target="tpu_custom_call" | custom-call | tf_op jit(solution)/shard_map/pallas_call | solution.py:568

commit v5 on v4

--- a/solution.py
+++ b/solution.py
@@ -9,7 +9,7 @@
 from jax.sharding import PartitionSpec as P
 
 LATE = (4, 5)
-UNROLL = 2
+UNROLL = 3
 MESH = pl.DeviceIdType.MESH
 F32 = jnp.float32
 BF16 = jnp.bfloat16

time: 69.9 us -> 69.7 us (level)
  no operation moved by 1% of the time
where the time goes in v5:
time: 69.7 us; the launch traced here: 69.5 us
  Pallas kernels  68.8 us (99%)
    pallas_call x1, Pallas kernels, per_device(): pl.pallas_call(functools.partial(kernel, sizes), out_shape=(jax.ShapeDtyp...  66.8 us
    pallas_call x1, Pallas kernels, per_device(): pl.pallas_call(write_out, out_shape=tuple((jax.ShapeDtypeStruct(x.shape,...  2.04 us

profile of v5, /device:TPU:1, one launch (start us, length us, event | category | flops | bytes accessed | tf_op | source)
XLA Modules:
  0.0 69.5 jit_solution(10532417082693982946)
XLA Ops:
  0.6 66.8 %shard_map.119 = (bf16[6,128,256]{2,1,0:T(8,128)(2,1)}, f32[6,128,128]{2,1,0:T(8,128)}, f32[128,256]{1,0:T(8,128)}, f32[128,256]{1,0:T(8,128)}, f32[1,256]{1,0:T(1,128)}) custom-call(bf16[24,128,128]{2,1,0:T(8,128)(2,1)} %bitcast.7, bf16[128,256]{1,0:T(8,128)(2,1)} %w_self_hbm.1, bf16[128,256]{1,0:T(8,128)(2,1)} %w_neigh_hbm.1, f32[1,256]{1,0:T(1,128)} %bitcast.10, ...), custom_call_target="tpu_custom_call" | custom-call | tf_op jit(solution)/shard_map/pallas_call | solution.py:543
  67.4 2.0 %shard_map.120 = (bf16[6,128,256]{2,1,0:T(8,128)(2,1)}, f32[6,128,128]{2,1,0:T(8,128)}, f32[128,256]{1,0:T(8,128)}, f32[128,256]{1,0:T(8,128)}, f32[1,256]{1,0:T(1,128)}) custom-call(bf16[6,128,256]{2,1,0:T(8,128)(2,1)} %get-tuple-element.15.refs_0_, f32[6,128,128]{2,1,0:T(8,128)} %get-tuple-element.16.refs_1_, f32[128,256]{1,0:T(8,128)} %get-tuple-element.17.refs_2_, ...), custom_call_target="tpu_custom_call" | custom-call | tf_op jit(solution)/shard_map/pallas_call | solution.py:568
